TPU v7x, 32 devices: a whole 2x2x4 slice. The times are simulated.
32 devices in a mesh: tm: 8 (over z, x), lm: 4 (over y, core).
Axes of the slice: x: 2, y: 2, z: 4, core: 2. Of those that a mesh axis runs over, the one named last changes fastest.
Arguments:
- camera_poses: float32 [6, 8192], P(None, 'tm'), may hold values from -1.5 to 1.5
- landmarks: float32 [3, 16384], P(None, ('tm', 'lm')), may hold values from -5 to 5
- odometry: float32 [6, 8192], P(None, 'tm'), may hold values from -1.5 to 1.5
- odometry_info: float32 [8192], P('tm'), may hold values from 100 to 3000
- observations: bfloat16 [3072, 3, 64, 64], P(('tm', 'lm')), may hold values from -6 to 6
- tile_frame: int32 [3072], P(('tm', 'lm')), may hold values from 0 to 15, as said below
- tile_block: int32 [3072], P(('tm', 'lm')), may hold values from 0 to 31, as said below
- tile_count: int32 [32], P(('tm', 'lm')), may hold values from 38 to 96, as said below
- block_slot: int32 [8, 32], P('tm'), may hold values from 0 to 31, each once within a row
Outputs:
- refined_poses: float32 [6, 8192], P(None, 'tm')
- refined_points: float32 [3, 16384], P(None, ('tm', 'lm'))
Inputs may be any that keep to these rules, and one draw needn't show every extreme that they name: `tile_frame`: frame blocks of the slot's own time shard. `tile_block`: landmark block ids of the slot's own time shard. `tile_count`: slots from this count on hold no live tile; some device is full. `block_slot`: each row is a permutation of the 32 block ids.
All inputs are finite; a program needn't handle non-finite values.
Results may differ from a plain program's by a relative error of at most 0.0003.
Values sent between devices are 32-bit elements; how exact they have to be, the bound alone decides.
A program may use at most 64 MiB of HBM per device.

v0:
```python
import jax
import jax.numpy as jnp
from jax import lax
from jax.sharding import PartitionSpec as P

TILE = 64
ITERS = 2


robust_scale = 4.0
damping = 1.0
moment_pairs = ((0, 0), (1, 1), (2, 2), (0, 1), (0, 2), (1, 2))


def extended_2(array, sides, width):
    for axis, dim in sides:
        count, length = (lax.axis_size(axis), array.shape[dim])
        up = [(i, (i + 1) % count) for i in range(count - 1)]
        down = [(j, i) for i, j in up]
        last = lax.slice_in_dim(array, length - width, length, axis=dim)
        initial = lax.slice_in_dim(array, 0, width, axis=dim)
        before = lax.ppermute(last, axis, up)
        after = lax.ppermute(initial, axis, down)
        array = jnp.concatenate([before, array, after], axis=dim)
    return array


def cross_product(left, right):
    return [
        left[1] * right[2] - left[2] * right[1],
        left[2] * right[0] - left[0] * right[2],
        left[0] * right[1] - left[1] * right[0],
    ]


def tile_terms(rotation, offset, points, measured_tiles, live_mask):
    rotation_rows = [rotation[k][:, :, None] for k in range(3)]
    offset_rows = [offset[k][:, :, None] for k in range(3)]
    point_columns = [points[k][:, None, :] for k in range(3)]
    measured = measured_tiles.astype(jnp.float32)
    turned = cross_product(rotation_rows, point_columns)
    residual = [point_columns[k] + turned[k] + offset_rows[k] - measured[:, k] for k in range(3)]
    squared = residual[0] * residual[0] + residual[1] * residual[1] + residual[2] * residual[2]
    weight = live_mask[:, None, None] / (1.0 + squared / robust_scale)
    weighted = [weight * residual[k] for k in range(3)]
    lever = cross_product(point_columns, weighted)
    frame_terms = [jnp.sum(lever[k], axis=2) for k in range(3)]
    frame_terms += [jnp.sum(weighted[k], axis=2) for k in range(3)]
    frame_terms += [jnp.sum(weight, axis=2)]
    frame_terms += [jnp.sum(weight * point_columns[k], axis=2) for k in range(3)]
    frame_terms += [
        jnp.sum(weight * (point_columns[a] * point_columns[b]), axis=2) for a, b in moment_pairs
    ]
    spun = cross_product(rotation_rows, weighted)
    point_terms = [jnp.sum(weighted[k] - spun[k], axis=1) for k in range(3)]
    rotation_square = (
        rotation_rows[0] * rotation_rows[0]
        + rotation_rows[1] * rotation_rows[1]
        + rotation_rows[2] * rotation_rows[2]
    )
    point_terms += [jnp.sum(weight * (1.0 + rotation_square), axis=1)]
    point_terms += [
        jnp.sum(weight * (rotation_rows[a] * rotation_rows[b]), axis=1) for a, b in moment_pairs
    ]
    return (jnp.stack(frame_terms, axis=1), jnp.stack(point_terms, axis=1))


def block_solve(matrix, vector):
    dimension = len(vector)
    factor = [[None] * dimension for i in range(dimension)]
    inverse_diag = [None] * dimension
    for i in range(dimension):
        for j in range(i + 1):
            running = matrix[i][j]
            for k in range(j):
                running = running - factor[i][k] * factor[j][k]
            if i == j:
                factor[i][i] = jnp.sqrt(running)
                inverse_diag[i] = 1.0 / factor[i][i]
            else:
                factor[i][j] = running * inverse_diag[j]
    forward = [None] * dimension
    for i in range(dimension):
        running = vector[i]
        for k in range(i):
            running = running - factor[i][k] * forward[k]
        forward[i] = running * inverse_diag[i]
    solution = [None] * dimension
    for i in reversed(range(dimension)):
        running = forward[i]
        for k in range(i + 1, dimension):
            running = running - factor[k][i] * solution[k]
        solution[i] = running * inverse_diag[i]
    return solution


def pose_step(sums, current, link_grad, link_diag):
    moments = [sums[10 + m] for m in range(6)]
    centroid = [sums[7 + m] for m in range(3)]
    counted = sums[6]
    diagonal_add = link_diag + damping
    zero_entry = jnp.zeros_like(counted)
    rotation_block = [
        [moments[1] + moments[2] + diagonal_add, -moments[3], -moments[4]],
        [-moments[3], moments[0] + moments[2] + diagonal_add, -moments[5]],
        [-moments[4], -moments[5], moments[0] + moments[1] + diagonal_add],
    ]
    cross_block = [
        [zero_entry, -centroid[2], centroid[1]],
        [centroid[2], zero_entry, -centroid[0]],
        [-centroid[1], centroid[0], zero_entry],
    ]
    matrix = []
    for i in range(3):
        matrix.append(rotation_block[i] + cross_block[i])
    for i in range(3):
        offset_row = [counted + diagonal_add if i == k else zero_entry for k in range(3)]
        matrix.append([cross_block[k][i] for k in range(3)] + offset_row)
    gradient = [sums[k] + link_grad[k] for k in range(6)]
    solution = block_solve(matrix, gradient)
    return current - jnp.stack(solution)


def point_step(sums, current):
    diagonal = sums[3] + damping
    outer = [sums[4 + m] for m in range(6)]
    matrix = [
        [diagonal - outer[0], -outer[3], -outer[4]],
        [-outer[3], diagonal - outer[1], -outer[5]],
        [-outer[4], -outer[5], diagonal - outer[2]],
    ]
    solution = block_solve(matrix, [sums[0], sums[1], sums[2]])
    return current - jnp.stack(solution)


def fetch_window(owned_points):
    return lax.all_gather(owned_points, "lm", axis=1, tiled=True)


def share_slice(array, share_start, share_width):
    return lax.dynamic_slice_in_dim(array, share_start, share_width, array.ndim - 1)


def share_update(share_sums, camera_poses, link_grad, link_diag, share_width):
    share_start = lax.axis_index("lm") * share_width
    new_share = pose_step(
        share_sums,
        share_slice(camera_poses, share_start, share_width),
        share_slice(link_grad, share_start, share_width),
        share_slice(link_diag, share_start, share_width),
    )
    return lax.all_gather(new_share, "lm", axis=1, tiled=True)


def on_device(
    camera_poses,
    landmarks,
    odometry,
    odometry_info,
    observations,
    tile_frame,
    tile_block,
    tile_count,
    block_slot,
):
    frames = camera_poses.shape[1]
    blocks = frames // TILE
    tile_slots = observations.shape[0]
    owner_count = lax.axis_size("lm")
    own_points = landmarks.shape[1]
    window_blocks = own_points * owner_count // TILE
    share_width = frames // owner_count
    live_mask = (jnp.arange(tile_slots) < tile_count[0]).astype(jnp.float32)
    positions = jnp.sum(
        jnp.where(
            tile_block[:, None] == jnp.arange(window_blocks)[None, :], block_slot[0][None, :], 0
        ),
        axis=1,
    )
    frame_onehot = (tile_frame[:, None] == jnp.arange(blocks)[None, :]).astype(jnp.float32)
    point_onehot = (positions[:, None] == jnp.arange(window_blocks)[None, :]).astype(jnp.float32)
    final_frame = (lax.axis_index("tm") == lax.axis_size("tm") - 1) & (
        jnp.arange(frames) == frames - 1
    )
    link_rows = jnp.concatenate([odometry, odometry_info[None, :]], axis=0)
    window = None
    for iteration in range(ITERS):
        window = fetch_window(landmarks)
        pose_blocks = camera_poses.reshape(6, blocks, TILE)
        picked = jnp.take(pose_blocks, tile_frame, axis=1)
        seen_points = jnp.take(window.reshape(3, window_blocks, TILE), positions, axis=1)
        frame_part, point_part = tile_terms(
            picked[0:3], picked[3:6], seen_points, observations, live_mask
        )
        frame_local = jnp.einsum(
            "tf,tqi->qfi", frame_onehot, frame_part, precision=lax.Precision.HIGHEST
        ).reshape(16, frames)
        point_local = jnp.einsum(
            "tp,tqi->qpi", point_onehot, point_part, precision=lax.Precision.HIGHEST
        ).reshape(10, window_blocks * TILE)
        extended = extended_2(jnp.concatenate([camera_poses, link_rows], axis=0), (("tm", 1),), 1)
        following = extended[0:6, 2:]
        previous = extended[0:6, :-2]
        motion_before = extended[6:12, :-2]
        weight_before = extended[12, :-2]
        weight_after = jnp.where(final_frame, 0.0, odometry_info)
        ahead_gap = following - camera_poses - odometry
        behind_gap = camera_poses - previous - motion_before
        link_grad = -weight_after[None, :] * ahead_gap + weight_before[None, :] * behind_gap
        link_diag = weight_after + weight_before
        share_sums = lax.psum_scatter(frame_local, "lm", scatter_dimension=1, tiled=True)
        next_poses = share_update(share_sums, camera_poses, link_grad, link_diag, share_width)
        owned_sums = lax.psum_scatter(point_local, "lm", scatter_dimension=1, tiled=True)
        landmarks = point_step(owned_sums, landmarks)
        window = None
        camera_poses = next_poses
    return (camera_poses, landmarks)


def solution(mesh):
    return jax.shard_map(
        on_device,
        mesh=mesh,
        in_specs=(
            P(None, "tm"),
            P(None, ("tm", "lm")),
            P(None, "tm"),
            P("tm"),
            P(("tm", "lm"), None, None, None),
            P(("tm", "lm")),
            P(("tm", "lm")),
            P(("tm", "lm")),
            P("tm", None),
        ),
        out_specs=(P(None, "tm"), P(None, ("tm", "lm"))),
        check_vma=False,
    )
```

profile of v0, /device:TPU:0, one launch (start us, length us, event | category | flops | bytes accessed | tf_op | source)
XLA Modules:
  0.0 177.9 jit_solution(16395414560604212685)
XLA Ops:
  9.8 6.4 %all_gather.12 = f32[3,2048]{1,0:T(4,128)S(1)} all-gather(f32[3,512]{1,0:T(4,128)} %param.14), channel_id=1, replica_groups=mesh['tm'=8,'lm'=4] {'lm'}, dimensions={1}, use_global_device_ids=true | all-gather | bytes 30720 | tf_op jit(solution)/shard_map/all_gather | solution.py:137
  23.7 1.5 fusion.74
  26.1 1.5 copy.173
  27.6 1.5 copy.174
  30.6 1.5 copy.176
  35.0 1.5 copy.179
  42.3 1.5 copy.170
  45.8 6.6 %multiply_reduce_fusion.16 = (f32[96,64]{0,1:T(8,128)S(1)}, f32[96,64]{0,1:T(8,128)S(1)}, f32[96,64]{0,1:T(8,128)S(1)}, f32[96,64]{0,1:T(8,128)S(1)}, f32[96,64]...) fusion(f32[96,64]{0,1:T(8,128)S(1)} %copy-done.15, ...), kind=kLoop, calls=%fused_computation.33 | loop fusion | flops 23095296 | bytes 7250304 | tf_op jit(solution)/shard_map/reduce_sum | solution.py:63
  52.4 1.9 %fusion.1 = (f32[96,64,64]{0,2,1:T(8,128)S(1)}, f32[96,64,64]{0,2,1:T(8,128)S(1)}, f32[96,64,64]{0,2,1:T(8,128)S(1)}) fusion(f32[96,64,64]{0,2,1:T(8,128)S(1)} %get-tuple-element.119, f32[96,3,64,64]{0,3,2,1:T(8,128)S(1)} %convert_element_type.14, f32[96,64]{0,1:T(8,128)S(1)} %copy.165, f32[96,64]{0,1:T(8,128)S(1)} %copy.164, f32[96,64]{0,1:T(8,128)S(1)} %copy.162, ...), kind=kLoop, calls=%fused_computation.60 | loop fusion | flops 8257536 | bytes 11231232 | tf_op jit(solution)/shard_map/mul | solution.py:45
  54.4 3.8 %subtract_reduce_fusion.6 = (f32[96,64]{0,1:T(8,128)S(1)}, f32[96,64]{0,1:T(8,128)S(1)}, f32[96,64]{0,1:T(8,128)S(1)}, f32[96,64]{0,1:T(8,128)S(1)}, f32[96,64]{...) fusion(f32[96,64,64]{0,2,1:T(8,128)S(1)} %get-tuple-element.125,, ...), kind=kLoop, calls=%fused_computation.40 | loop fusion | flops 11741184 | bytes 5087232 | tf_op jit(solution)/shard_map/reduce_sum | solution.py:55
  60.1 3.8 %collective-permute-start.1 = (f32[13,1]{1,0:T(8,128)S(1)}, f32[13,1]{1,0:T(8,128)S(1)}, u32[]{:S(2)}, u32[]{:S(2)}) collective-permute-start(f32[13,1]{1,0:T(8,128)S(1)} %get-tuple-element.173), channel_id=1, source_target_pairs={{0,4},{4,8},{8,12},{12,16},{16,20},{20,24},{24,28},{1,5},{5,9},{9,... | collective-permute-start | bytes 164 | tf_op jit(solution)/shard_map/ppermute | solution.py:22
  67.1 2.4 %collective-permute-done = f32[13,1]{1,0:T(8,128)S(1)} collective-permute-done((f32[13,1]{1,0:T(8,128)S(1)}, f32[13,1]{1,0:T(8,128)S(1)}, u32[]{:S(2)}, u32[]{:S(2)}) %collective-permute-start) | collective-permute-done | bytes 84 | tf_op jit(solution)/shard_map/ppermute | solution.py:23
  69.6 11.7 %reduce-scatter.5.cloned.1.call-done = f32[16,256]{1,0:T(8,128)} async-done(((f32[16,1024]{1,0:T(8,128)}), f32[16,256]{1,0:T(8,128)}) %reduce-scatter.5.cloned.1.call-update) | async-done | bytes 16400 | tf_op jit(solution)/shard_map/reduce_scatter | solution.py:211
  83.3 5.2 %all_gather.13 = f32[6,1024]{1,0:T(8,128)S(1)} all-gather(f32[6,256]{1,0:T(8,128)S(1)} %dynamic-slice_subtract_fusion.5), channel_id=1, replica_groups=mesh['tm'=8,'lm'=4] {'lm'}, dimensions={1}, use_global_device_ids=true | all-gather | bytes 30720 | tf_op jit(solution)/shard_map/all_gather | solution.py:152
  90.7 3.4 %collective-permute-start.3 = (f32[13,1]{1,0:T(8,128)S(1)}, f32[13,1]{1,0:T(8,128)S(1)}, u32[]{:S(2)}, u32[]{:S(2)}) collective-permute-start(f32[13,1]{1,0:T(8,128)S(1)} %get-tuple-element.171), channel_id=1, source_target_pairs={{0,4},{4,8},{8,12},{12,16},{16,20},{20,24},{24,28},{1,5},{5,9},{9,... | collective-permute-start | bytes 164 | tf_op jit(solution)/shard_map/ppermute | solution.py:22
  95.7 4.0 %collective-permute-done.2 = f32[13,1]{1,0:T(8,128)S(1)} collective-permute-done((f32[13,1]{1,0:T(8,128)S(1)}, f32[13,1]{1,0:T(8,128)S(1)}, u32[]{:S(2)}, u32[]{:S(2)}) %collective-permute-start.2) | collective-permute-done | bytes 84 | tf_op jit(solution)/shard_map/ppermute | solution.py:23
  99.7 3.8 %reduce-scatter.7.cloned.1.call-done = f32[10,512]{1,0:T(8,128)} async-done(((f32[10,2048]{1,0:T(8,128)}), f32[10,512]{1,0:T(8,128)}) %reduce-scatter.7.cloned.1.call-update) | async-done | bytes 20496 | tf_op jit(solution)/shard_map/reduce_scatter | solution.py:213
  104.6 5.4 %all_gather.14 = f32[3,2048]{1,0:T(4,128)S(1)} all-gather(f32[3,512]{1,0:T(4,128)S(1)} %maximum_subtract_fusion), channel_id=1, replica_groups=mesh['tm'=8,'lm'=4] {'lm'}, dimensions={1}, use_global_device_ids=true | all-gather | bytes 30720 | tf_op jit(solution)/shard_map/all_gather | solution.py:137
  111.9 8.1 %multiply_reduce_fusion = (f32[96,64]{0,1:T(8,128)S(1)}, f32[96,64]{0,1:T(8,128)S(1)}, f32[96,64]{0,1:T(8,128)S(1)}, f32[96,64]{0,1:T(8,128)S(1)}, f32[96,64]{0,...) fusion(f32[96,64]{0,1:T(8,128)S(1)} %copy.206, ...), kind=kLoop, calls=%fused_computation.7 | loop fusion | flops 23095296 | bytes 7250304 | tf_op jit(solution)/shard_map/reduce_sum | solution.py:63
  120.0 1.9 %fusion.4 = (f32[96,64,64]{0,2,1:T(8,128)S(1)}, f32[96,64,64]{0,2,1:T(8,128)S(1)}, f32[96,64,64]{0,2,1:T(8,128)S(1)}) fusion(f32[96,64,64]{0,2,1:T(8,128)S(1)} %get-tuple-element.87, f32[96,3,64,64]{0,3,2,1:T(8,128)S(1)} %bitcast.291, f32[96,64]{0,1:T(8,128)S(1)} %copy.192, f32[96,64]{0,1:T(8,128)S(1)} %copy.191, f32[96,64]{0,1:T(8,128)S(1)} %copy.189, ...), kind=kLoop, calls=%fused_computation.63 | loop fusion | flops 8257536 | bytes 11231232 | tf_op jit(solution)/shard_map/mul | solution.py:45
  121.9 3.8 %subtract_reduce_fusion = (f32[96,64]{0,1:T(8,128)S(1)}, f32[96,64]{0,1:T(8,128)S(1)}, f32[96,64]{0,1:T(8,128)S(1)}, f32[96,64]{0,1:T(8,128)S(1)}, f32[96,64]{0,...) fusion(f32[96,64,64]{0,2,1:T(8,128)S(1)} %get-tuple-element.122, ...), kind=kLoop, calls=%fused_computation.14 | loop fusion | flops 11741184 | bytes 5087232 | tf_op jit(solution)/shard_map/reduce_sum | solution.py:55
  129.0 18.1 %reduce-scatter.9.cloned.1.call-done = f32[16,256]{1,0:T(8,128)} async-done(((f32[16,1024]{1,0:T(8,128)}), f32[16,256]{1,0:T(8,128)}) %reduce-scatter.9.cloned.1.call-update) | async-done | bytes 16400 | tf_op jit(solution)/shard_map/reduce_scatter | solution.py:211
  149.1 5.2 %all_gather.15 = f32[6,1024]{1,0:T(8,128)S(1)} all-gather(f32[6,256]{1,0:T(8,128)S(1)} %dynamic-slice_subtract_fusion.4), channel_id=1, replica_groups=mesh['tm'=8,'lm'=4] {'lm'}, dimensions={1}, use_global_device_ids=true | all-gather | bytes 30720 | tf_op jit(solution)/shard_map/all_gather | solution.py:152
  154.3 14.8 %reduce-scatter.11.cloned.1.call-done = f32[10,512]{1,0:T(8,128)} async-done(((f32[10,2048]{1,0:T(8,128)}), f32[10,512]{1,0:T(8,128)}) %reduce-scatter.11.cloned.1.call-update) | async-done | bytes 20496 | tf_op jit(solution)/shard_map/reduce_scatter | solution.py:213
  (235 shorter events, 43.2 us)
Async XLA Ops:
  7.2 74.1 %reduce-scatter.5.cloned.1.call-start = ((), (), s32[]{:S(2)}) async-start(), calls=%async_computation.4 | async-start | bytes 81920 | tf_op jit(solution)/shard_map/reduce_scatter | solution.py:211
  18.0 2.0 %copy-start.3 = (f32[1,96,64]{2,0,1:T(1,128)}, f32[1,96,64]{2,0,1:T(1,128)S(1)}, u32[]{:S(2)}) copy-start(f32[1,96,64]{2,0,1:T(1,128)S(1)} %get-tuple-element.148) | copy-start | bytes 73732
  18.0 2.0 %copy-start.4 = (f32[1,96,64]{2,0,1:T(1,128)}, f32[1,96,64]{2,0,1:T(1,128)S(1)}, u32[]{:S(2)}) copy-start(f32[1,96,64]{2,0,1:T(1,128)S(1)} %get-tuple-element.149) | copy-start | bytes 73732
  21.5 22.5 %copy-start.1 = (bf16[96,3,64,64]{0,3,2,1:T(8,128)(2,1)S(1)}, bf16[96,3,64,64]{0,3,2,1:T(8,128)(2,1)}, u32[]{:S(2)}) copy-start(bf16[96,3,64,64]{0,3,2,1:T(8,128)(2,1)} %param.17) | copy-start | bytes 7077892
  44.1 1.6 copy-start.6
  44.1 1.6 copy-start.7
  44.1 1.6 copy-start.9
  44.1 1.6 copy-start.10
  45.0 7.5 %copy-start = (f32[96,3,64,64]{0,3,2,1:T(8,128)}, f32[96,3,64,64]{0,3,2,1:T(8,128)S(1)}, u32[]{:S(2)}) copy-start(f32[96,3,64,64]{0,3,2,1:T(8,128)S(1)} %convert_element_type.14) | copy-start | bytes 14155780
  54.3 4.1 %copy-start.24 = (s32[96]{0:T(128)S(1)}, s32[96]{0:T(128)}, u32[]{:S(2)}) copy-start(s32[96]{0:T(128)} %param.18) | copy-start | bytes 1156
  54.3 5.6 %copy-start.2 = (f32[6,1024]{1,0:T(8,128)S(1)}, f32[6,1024]{1,0:T(8,128)}, u32[]{:S(2)}) copy-start(f32[6,1024]{1,0:T(8,128)} %param.15) | copy-start | bytes 73732
  54.3 5.6 %copy-start.5 = (f32[6,1024]{1,0:T(8,128)S(1)}, f32[6,1024]{1,0:T(8,128)}, u32[]{:S(2)}) copy-start(f32[6,1024]{1,0:T(8,128)} %param.13) | copy-start | bytes 73732
  54.4 5.6 %copy-start.8 = (f32[1024]{0:T(1024)S(1)}, f32[1024]{0:T(1024)}, u32[]{:S(2)}) copy-start(f32[1024]{0:T(1024)} %param.16) | copy-start | bytes 12292
  58.4 30.9 %copy-start.23 = (pred[96]{0:T(512)(128)(4,1)S(1)}, pred[96]{0:T(512)(128)(4,1)}, u32[]{:S(2)}) copy-start(pred[96]{0:T(512)(128)(4,1)} %get-tuple-element.220) | copy-start | bytes 292
  59.9 43.6 %reduce-scatter.7.cloned.1.call-start = ((), (), s32[]{:S(2)}) async-start(), calls=%async_computation.5 | async-start | bytes 163840 | tf_op jit(solution)/shard_map/reduce_scatter | solution.py:213
  60.1 6.7 %collective-permute-start.1 = (f32[13,1]{1,0:T(8,128)S(1)}, f32[13,1]{1,0:T(8,128)S(1)}, u32[]{:S(2)}, u32[]{:S(2)}) collective-permute-start(f32[13,1]{1,0:T(8,128)S(1)} %get-tuple-element.173), channel_id=1, source_target_pairs={{0,4},{4,8},{8,12},{12,16},{16,20},{20,24},{24,28},{1,5},{5,9},{9,... | collective-permute-start | bytes 164 | tf_op jit(solution)/shard_map/ppermute | solution.py:22
  63.9 5.5 %collective-permute-start = (f32[13,1]{1,0:T(8,128)S(1)}, f32[13,1]{1,0:T(8,128)S(1)}, u32[]{:S(2)}, u32[]{:S(2)}) collective-permute-start(f32[13,1]{1,0:T(8,128)S(1)} %get-tuple-element.172), channel_id=1, source_target_pairs={{4,0},{8,4},{12,8},{16,12},{20,16},{24,20},{28,24},{5,1},{9,5},{13... | collective-permute-start | bytes 164 | tf_op jit(solution)/shard_map/ppermute | solution.py:23
  66.7 80.3 %reduce-scatter.9.cloned.1.call-start = ((), (), s32[]{:S(2)}) async-start(), calls=%async_computation.6 | async-start | bytes 81920 | tf_op jit(solution)/shard_map/reduce_scatter | solution.py:211
  88.6 15.9 %copy-start.22 = (f32[3,512]{1,0:T(4,128)S(1)}, f32[3,512]{1,0:T(4,128)}, u32[]{:S(2)}) copy-start(f32[3,512]{1,0:T(4,128)} %param.14) | copy-start | bytes 18436
  90.7 4.7 %collective-permute-start.3 = (f32[13,1]{1,0:T(8,128)S(1)}, f32[13,1]{1,0:T(8,128)S(1)}, u32[]{:S(2)}, u32[]{:S(2)}) collective-permute-start(f32[13,1]{1,0:T(8,128)S(1)} %get-tuple-element.171), channel_id=1, source_target_pairs={{0,4},{4,8},{8,12},{12,16},{16,20},{20,24},{24,28},{1,5},{5,9},{9,... | collective-permute-start | bytes 164 | tf_op jit(solution)/shard_map/ppermute | solution.py:22
  94.1 5.5 %collective-permute-start.2 = (f32[13,1]{1,0:T(8,128)S(1)}, f32[13,1]{1,0:T(8,128)S(1)}, u32[]{:S(2)}, u32[]{:S(2)}) collective-permute-start(f32[13,1]{1,0:T(8,128)S(1)} %get-tuple-element.170), channel_id=1, source_target_pairs={{4,0},{8,4},{12,8},{16,12},{20,16},{24,20},{28,24},{5,1},{9,5},{13... | collective-permute-start | bytes 164 | tf_op jit(solution)/shard_map/ppermute | solution.py:23
  110.8 9.2 %slice-start = ((s8[6291456]{0:T(1024)(128)(4,1)}), s8[2097152]{0:T(1024)(128)(4,1)S(1)}, s32[]{:S(2)}) async-start(s8[6291456]{0:T(1024)(128)(4,1)} %bitcast.290), calls=%async_computation.8 | async-start | bytes 4194304
  111.9 8.2 %slice-start.1 = ((s8[6291456]{0:T(1024)(128)(4,1)}), s8[4194304]{0:T(1024)(128)(4,1)S(1)}, s32[]{:S(2)}) async-start(s8[6291456]{0:T(1024)(128)(4,1)} %bitcast.290), calls=%async_computation.9 | async-start | bytes 8388608
  127.5 41.6 %reduce-scatter.11.cloned.1.call-start = ((), (), s32[]{:S(2)}) async-start(), calls=%async_computation.7 | async-start | bytes 163840 | tf_op jit(solution)/shard_map/reduce_scatter | solution.py:213
  (11 other events, 17.3 us)
Sparse Core Ops, SparseCore 0:
  60.0 21.1 reduce-scatter.4
  83.8 19.6 reduce-scatter.6
  127.6 19.4 reduce-scatter.8
  149.5 19.5 reduce-scatter.10
where the time goes:
time: 179 us; the launch traced here: 178 us
  waiting for transfers between devices  54.8 us (31%)
  other arithmetic  41.1 us (23%)
  local copies, waits for them, and re-layouts  31.7 us (18%)
  blocking collectives  22.2 us (12%)
  between operations  15.6 us (9%)
  starting transfers between devices  9.93 us (6%)
  matrix products  2.62 us (1%)
    reduce_scatter x2, waiting for transfers between devices, on_device(): lax.psum_scatter(frame_local, 'lm', scatter_dimension=1, tiled=True)  29.8 us
    reduce_scatter x2, waiting for transfers between devices, on_device(): lax.psum_scatter(point_local, 'lm', scatter_dimension=1, tiled=True)  18.6 us
    reduce_sum x2, other arithmetic, tile_terms(): jnp.sum(weight * (rotation_rows[a] * rotation_rows[b]), axis=1)  14.7 us
    all_gather x2, blocking collectives, fetch_window(): return lax.all_gather(owned_points, 'lm', axis=1, tiled=True)  11.8 us
    all_gather x2, blocking collectives, share_update(): return lax.all_gather(new_share, 'lm', axis=1, tiled=True)  10.4 us
    mul x12, local copies, waits for them, and re-layouts, tile_terms(): point_columns[a] * point_columns[b]  7.8 us
    reduce_sum x2, other arithmetic, tile_terms(): point_terms = [jnp.sum(weighted[k] - spun[k], axis=1) for k in range(3)]  7.65 us
    ppermute x2, starting transfers between devices, extended_2(): before = lax.ppermute(last, axis, up)  7.18 us
  transfers between devices with their start and end apart: 8, of which 6 were waited for; matrix products, arithmetic and copies ran while one was open for 5% of the time, Pallas kernels for 0%

commit v1 on v0

v1 whole, which is shorter than its diff:
```python
import functools

import jax
import jax.numpy as jnp
from jax import lax
from jax.experimental import pallas as pl
from jax.experimental.pallas import tpu as pltpu
from jax.sharding import PartitionSpec as P

TILE = 64
HALF = 32
ITERS = 2
MESH = pl.DeviceIdType.MESH

robust_scale = 4.0
damping = 1.0
moment_pairs = ((0, 0), (1, 1), (2, 2), (0, 1), (0, 2), (1, 2))


def cross_product(left, right):
    return [
        left[1] * right[2] - left[2] * right[1],
        left[2] * right[0] - left[0] * right[2],
        left[0] * right[1] - left[1] * right[0],
    ]


def block_solve(matrix, vector):
    dimension = len(vector)
    factor = [[None] * dimension for i in range(dimension)]
    inverse_diag = [None] * dimension
    for i in range(dimension):
        for j in range(i + 1):
            running = matrix[i][j]
            for k in range(j):
                running = running - factor[i][k] * factor[j][k]
            if i == j:
                factor[i][i] = jnp.sqrt(running)
                inverse_diag[i] = 1.0 / factor[i][i]
            else:
                factor[i][j] = running * inverse_diag[j]
    forward = [None] * dimension
    for i in range(dimension):
        running = vector[i]
        for k in range(i):
            running = running - factor[i][k] * forward[k]
        forward[i] = running * inverse_diag[i]
    solution = [None] * dimension
    for i in reversed(range(dimension)):
        running = forward[i]
        for k in range(i + 1, dimension):
            running = running - factor[k][i] * solution[k]
        solution[i] = running * inverse_diag[i]
    return solution


def split_rows(value):
    high = value.astype(jnp.bfloat16)
    low = (value - high.astype(jnp.float32)).astype(jnp.bfloat16)
    return high, low


def tiles_kernel(
    tile_frame,
    tile_block,
    tile_count,
    block_slot,
    poses,
    window,
    obs,
    frame_out,
    point_out,
    pose_wide,
    point_wide,
    frame_feat,
    point_feat,
    build_frame,
    build_point,
    frame_acc,
    point_acc,
):
    step = pl.program_id(0)
    frame_blocks = poses.shape[0]
    point_blocks = window.shape[0]
    step_tiles = obs.shape[0]
    lane = lax.broadcasted_iota(jnp.int32, (1, 128), 1)
    upper = lane >= TILE

    @pl.when(step == 0)
    def _():
        frame_acc[...] = jnp.zeros_like(frame_acc)
        point_acc[...] = jnp.zeros_like(point_acc)
        build_frame[...] = jnp.zeros_like(build_frame)
        build_point[...] = jnp.zeros_like(build_point)

        @pl.loop(0, frame_blocks)
        def _(block):
            columns = jnp.transpose(poses[block, 0:8, :])
            for k in range(6):
                column = columns[:, k : k + 1]
                pose_wide[block, k] = jnp.where(
                    upper,
                    jnp.broadcast_to(column[HALF:], (HALF, 128)),
                    jnp.broadcast_to(column[:HALF], (HALF, 128)),
                )

        image = lane // HALF
        for half in range(2):
            value = []
            for k in range(6):
                part = poses[:, k, :][:, half * HALF : (half + 1) * HALF]
                value.append(jnp.concatenate([part] * 4, axis=1))
            w, t = value[0:3], value[3:6]
            turned = cross_product(w, t)
            zero = jnp.zeros_like(w[0])
            rows = []
            for m in range(3):
                a, b = (m + 1) % 3, (m + 2) % 3
                coefs = [t[m] - turned[m], zero, zero, zero]
                coefs[1 + m] = zero - 1.0
                coefs[1 + b] = w[a]
                coefs[1 + a] = -w[b]
                row = coefs[0]
                for g in range(1, 4):
                    row = jnp.where(image == g, coefs[g], row)
                rows.append(row)
            first = image == 0
            square = w[0] * w[0] + w[1] * w[1] + w[2] * w[2]
            rows.append(jnp.where(first, 1.0 + square, 0.0))
            for a, b in moment_pairs:
                rows.append(jnp.where(first, w[a] * w[b], 0.0))
            for q, row in enumerate(rows):
                build_frame[:, half * 16 + q, :] = row

        spread = []
        for k in range(3):
            part = window[:, k, :]
            spread.append(jnp.concatenate([part, part], axis=1))
            point_wide[:, k, :] = spread[k]
        one = jnp.ones_like(spread[0])
        features = [one] + spread
        moments = [spread[a] * spread[b] for a, b in moment_pairs]
        for half in range(2):
            mine = upper if half else jnp.logical_not(upper)
            for f, feature in enumerate(features):
                build_point[:, half * 20 + f, :] = jnp.where(mine, feature, 0.0)
            for f, feature in enumerate(moments):
                build_point[:, half * 16 + 8 + f, :] = jnp.where(mine, feature, 0.0)

        @pl.loop(0, frame_blocks)
        def _(block):
            high, low = split_rows(build_frame[block])
            frame_feat[block, 0:32, :] = high
            frame_feat[block, 32:64, :] = low

        @pl.loop(0, point_blocks)
        def _(block):
            high, low = split_rows(build_point[block])
            point_feat[block, 0:32, :] = high
            point_feat[block, 32:64, :] = low

    def one_tile(t, slot):
        f = tile_frame[slot]
        p = block_slot[0, tile_block[slot]]
        measured = obs[t]
        measured = jnp.concatenate(
            [measured[:, :HALF, :], measured[:, HALF:, :]], axis=2
        ).astype(jnp.float32)
        x = [point_wide[p, k : k + 1, :] for k in range(3)]
        w = [pose_wide[f, k] for k in range(3)]
        turned = cross_product(w, x)
        residual = [
            x[k] + turned[k] + pose_wide[f, 3 + k] - measured[k] for k in range(3)
        ]
        squared = (
            residual[0] * residual[0] + residual[1] * residual[1] + residual[2] * residual[2]
        )
        weight = 1.0 / (1.0 + squared * (1.0 / robust_scale))
        images = jnp.concatenate(
            [weight] + [weight * measured[k] for k in range(3)], axis=0
        )
        high, low = split_rows(images)
        g = frame_feat[f]
        with_high = lax.dot_general(
            g, high, (((1,), (0,)), ((), ())), preferred_element_type=jnp.float32
        )
        with_low = lax.dot_general(
            g[0:32], low, (((1,), (0,)), ((), ())), preferred_element_type=jnp.float32
        )
        point_acc[p] += with_high[0:32] + with_high[32:64] + with_low
        h = point_feat[p]
        with_high = lax.dot_general(
            h, high, (((1,), (1,)), ((), ())), preferred_element_type=jnp.float32
        )
        with_low = lax.dot_general(
            h[0:32], low, (((1,), (1,)), ((), ())), preferred_element_type=jnp.float32
        )
        frame_acc[f] += with_high[0:32] + with_high[32:64] + with_low

    here = jnp.clip(tile_count[0] - step * step_tiles, 0, step_tiles)

    @pl.loop(0, here)
    def _(t):
        one_tile(t, step * step_tiles + t)

    @pl.when(step == pl.num_programs(0) - 1)
    def _():
        @pl.loop(0, frame_blocks)
        def _(block):
            total = frame_acc[block]
            frame_out[block, 0:8, :] = total[0:8] + total[16:24]
            frame_out[block, 8:16, :] = jnp.where(
                lane < HALF, total[8:16], pltpu.roll(total[24:32], HALF, 1)
            )

        @pl.loop(0, point_blocks)
        def _(block):
            total = point_acc[block]
            point_out[block] = jnp.where(
                upper,
                pltpu.roll(total[8:16], TILE, 1) + total[24:32],
                total[0:8] + pltpu.roll(total[16:24], TILE, 1),
            )


def tile_sums(poses, window, observations, tile_frame, tile_block, tile_count, block_slot):
    slots = observations.shape[0]
    frame_blocks, point_blocks = poses.shape[0], window.shape[0]
    steps = 4
    while slots % steps:
        steps -= 1
    whole = lambda shape: pl.BlockSpec(shape, lambda s, *_: (0,) * len(shape))
    grid_spec = pltpu.PrefetchScalarGridSpec(
        num_scalar_prefetch=4,
        grid=(steps,),
        in_specs=[
            whole(poses.shape),
            whole(window.shape),
            pl.BlockSpec((slots // steps, 3, TILE, TILE), lambda s, *_: (s, 0, 0, 0)),
        ],
        out_specs=[whole((frame_blocks, 16, 128)), whole((point_blocks, 8, 128))],
        scratch_shapes=[
            pltpu.VMEM((frame_blocks, 6, HALF, 128), jnp.float32),
            pltpu.VMEM((point_blocks, 8, 128), jnp.float32),
            pltpu.VMEM((frame_blocks, 64, 128), jnp.bfloat16),
            pltpu.VMEM((point_blocks, 64, 128), jnp.bfloat16),
            pltpu.VMEM((frame_blocks, 32, 128), jnp.float32),
            pltpu.VMEM((point_blocks, 32, 128), jnp.float32),
            pltpu.VMEM((frame_blocks, 32, 128), jnp.float32),
            pltpu.VMEM((point_blocks, 32, 128), jnp.float32),
        ],
    )
    return pl.pallas_call(
        tiles_kernel,
        grid_spec=grid_spec,
        out_shape=[
            jax.ShapeDtypeStruct((frame_blocks, 16, 128), jnp.float32),
            jax.ShapeDtypeStruct((point_blocks, 8, 128), jnp.float32),
        ],
        compiler_params=pltpu.CompilerParams(vmem_limit_bytes=48 * 1024 * 1024),
        name="tile_sums",
    )(tile_frame, tile_block, tile_count, block_slot, poses, window, observations)


def ring_peers(count):
    me = lax.axis_index("lm")
    return me, [lax.rem(me + d, count) for d in range(1, count)]


def greet(peers, row, rows):
    barrier = pltpu.get_barrier_semaphore()
    for peer in peers:
        pl.semaphore_signal(barrier, inc=1, device_id=(row, peer), device_id_type=MESH)
    if rows is None:
        pl.semaphore_wait(barrier, len(peers))
        return
    me = lax.axis_index("lm")

    @pl.when(row > 0)
    def _():
        pl.semaphore_signal(barrier, inc=1, device_id=(row - 1, me), device_id_type=MESH)

    @pl.when(row < rows - 1)
    def _():
        pl.semaphore_signal(barrier, inc=1, device_id=(row + 1, me), device_id_type=MESH)

    edges = jnp.minimum(row, 1) + jnp.minimum(rows - 1 - row, 1)
    pl.semaphore_wait(barrier, len(peers) + edges)


def gather_kernel(count, own, window, send_sem, recv_sem):
    row = lax.axis_index("tm")
    me, peers = ring_peers(count)
    blocks = own.shape[0]
    greet(peers, row, None)
    copies = []
    for d, peer in enumerate(peers):
        copies.append(
            pltpu.make_async_remote_copy(
                src_ref=own,
                dst_ref=window.at[pl.ds(me * blocks, blocks)],
                send_sem=send_sem.at[d],
                recv_sem=recv_sem.at[d],
                device_id=(row, peer),
                device_id_type=MESH,
            )
        )
        copies[-1].start()
    window[pl.ds(me * blocks, blocks)] = own[...]
    for copy in copies:
        copy.wait()


def gather_points(own, count):
    blocks = own.shape[0]
    vmem = pl.BlockSpec(memory_space=pltpu.VMEM)
    return pl.pallas_call(
        functools.partial(gather_kernel, count),
        out_shape=jax.ShapeDtypeStruct((blocks * count,) + own.shape[1:], jnp.float32),
        in_specs=[vmem],
        out_specs=vmem,
        scratch_shapes=[
            pltpu.SemaphoreType.DMA((count - 1,)),
            pltpu.SemaphoreType.DMA((count - 1,)),
        ],
        compiler_params=pltpu.CompilerParams(collective_id=0, has_side_effects=True),
        name="gather_points",
    )(own)


def pose_update(total, state, before, after, final):
    def both(row_low, row_high, start):
        return jnp.concatenate(
            [total[:, row_low, start : start + HALF], total[:, row_high, start : start + HALF]],
            axis=1,
        )

    counted = both(0, 4, 0)
    centroid = [both(1 + k, 5 + k, 0) for k in range(3)]
    moments = [total[:, 8 + m, 0:TILE] for m in range(6)]
    seen = [both(0, 4, HALF * (1 + k)) for k in range(3)]

    def lever(a, k):
        return both(1 + a, 5 + a, HALF * (1 + k))

    current = [state[:, k, :] for k in range(6)]
    w, t = current[0:3], current[3:6]
    turned = cross_product(w, centroid)
    grad_off = [centroid[k] + turned[k] + t[k] * counted - seen[k] for k in range(3)]
    matrix_rows = [
        [moments[0], moments[3], moments[4]],
        [moments[3], moments[1], moments[5]],
        [moments[4], moments[5], moments[2]],
    ]
    trace = moments[0] + moments[1] + moments[2]
    pushed = cross_product(centroid, t)
    grad_rot = []
    for k in range(3):
        a, b = (k + 1) % 3, (k + 2) % 3
        product = (
            matrix_rows[k][0] * w[0] + matrix_rows[k][1] * w[1] + matrix_rows[k][2] * w[2]
        )
        grad_rot.append(trace * w[k] - product + pushed[k] - (lever(a, b) - lever(b, a)))

    weight_before = before[:, 12, :]
    weight_after = jnp.where(final, 0.0, state[:, 12, :])
    link_grad = []
    for k in range(6):
        ahead = after[:, k, :] - current[k] - state[:, 6 + k, :]
        behind = current[k] - before[:, k, :] - before[:, 6 + k, :]
        link_grad.append(weight_before * behind - weight_after * ahead)
    diagonal_add = weight_after + weight_before + damping

    zero_entry = jnp.zeros_like(counted)
    rotation_block = [
        [moments[1] + moments[2] + diagonal_add, -moments[3], -moments[4]],
        [-moments[3], moments[0] + moments[2] + diagonal_add, -moments[5]],
        [-moments[4], -moments[5], moments[0] + moments[1] + diagonal_add],
    ]
    cross_block = [
        [zero_entry, -centroid[2], centroid[1]],
        [centroid[2], zero_entry, -centroid[0]],
        [-centroid[1], centroid[0], zero_entry],
    ]
    matrix = [rotation_block[i] + cross_block[i] for i in range(3)]
    for i in range(3):
        offset_row = [counted + diagonal_add if i == k else zero_entry for k in range(3)]
        matrix.append([cross_block[k][i] for k in range(3)] + offset_row)
    sums = grad_rot + grad_off
    step = block_solve(matrix, [sums[k] + link_grad[k] for k in range(6)])
    return [current[k] - step[k] for k in range(6)]


def point_update(total, own):
    x = [own[:, k, :] for k in range(3)]
    spread = total[:, 3, 0:TILE]
    outer = [total[:, 4 + m, 0:TILE] for m in range(4)]
    outer += [total[:, m, TILE:] for m in range(2)]
    rows = [
        [outer[0], outer[3], outer[4]],
        [outer[3], outer[1], outer[5]],
        [outer[4], outer[5], outer[2]],
    ]
    gradient = [
        total[:, k, 0:TILE]
        + spread * x[k]
        - (rows[k][0] * x[0] + rows[k][1] * x[1] + rows[k][2] * x[2])
        for k in range(3)
    ]
    diagonal = spread + damping
    matrix = [
        [diagonal - outer[0], -outer[3], -outer[4]],
        [-outer[3], diagonal - outer[1], -outer[5]],
        [-outer[4], -outer[5], diagonal - outer[2]],
    ]
    step = block_solve(matrix, gradient)
    return [x[k] - step[k] for k in range(3)]


def exchange_kernel(
    count,
    rows,
    last,
    frame_sums,
    point_sums,
    state,
    own,
    new_state,
    new_points,
    frame_in,
    point_in,
    edge_in,
    extended,
    send_sem,
    recv_sem,
    edge_send,
    edge_recv,
):
    row = lax.axis_index("tm")
    me, peers = ring_peers(count)
    frame_blocks = state.shape[0]
    share = frame_blocks // count
    own_blocks = own.shape[0]
    greet(peers, row, rows)

    def send(group, d, peer, source, target):
        copy = pltpu.make_async_remote_copy(
            src_ref=source,
            dst_ref=target,
            send_sem=send_sem.at[group, d],
            recv_sem=recv_sem.at[group, d],
            device_id=(row, peer),
            device_id_type=MESH,
        )
        copy.start()
        return copy

    def edge(side, target_row):
        block = frame_blocks - 1 if side == 0 else 0
        return pltpu.make_async_remote_copy(
            src_ref=state.at[block],
            dst_ref=edge_in.at[side],
            send_sem=edge_send.at[side],
            recv_sem=edge_recv.at[side],
            device_id=(target_row, me),
            device_id_type=MESH,
        )

    frame_copies = [
        send(0, d, peer, frame_sums.at[pl.ds(peer * share, share)], frame_in.at[d])
        for d, peer in enumerate(peers)
    ]

    @pl.when(row < rows - 1)
    def _():
        edge(0, row + 1).start()

    @pl.when(row > 0)
    def _():
        edge(1, row - 1).start()

    point_copies = [
        send(1, d, peer, point_sums.at[pl.ds(peer * own_blocks, own_blocks)], point_in.at[d])
        for d, peer in enumerate(peers)
    ]

    extended[pl.ds(1, frame_blocks)] = state[...]
    extended[0] = jnp.zeros_like(extended[0])
    extended[frame_blocks + 1] = jnp.zeros_like(extended[0])

    @pl.when(row > 0)
    def _():
        edge(0, row - 1).wait_recv()
        extended[0] = edge_in[0]

    @pl.when(row < rows - 1)
    def _():
        edge(1, row + 1).wait_recv()
        extended[frame_blocks + 1] = edge_in[1]

    first = me * share
    mine = state[pl.ds(first, share)]
    ahead = extended[pl.ds(first + 2, share)]
    behind = extended[pl.ds(first, share)]
    after = jnp.concatenate([mine[:, :, 1:], ahead[:, :, :1]], axis=2)
    before = jnp.concatenate([behind[:, :, TILE - 1 :], mine[:, :, : TILE - 1]], axis=2)
    block_index = lax.broadcasted_iota(jnp.int32, (share, TILE), 0) + first
    lane = lax.broadcasted_iota(jnp.int32, (share, TILE), 1)
    final = (block_index * TILE + lane) == jnp.where(
        row == rows - 1, frame_blocks * TILE - 1, -1
    )

    total = frame_sums[pl.ds(first, share)]
    for d, copy in enumerate(frame_copies):
        copy.wait_recv()
        total = total + frame_in[d]
    poses = pose_update(total, mine, before, after, final)
    here = pl.ds(first, share)
    new_state[here] = mine
    for k in range(6):
        new_state[here, k, :] = poses[k]
    pose_copies = [
        send(2, d, peer, new_state.at[here], new_state.at[here])
        for d, peer in enumerate(peers)
    ]

    total = point_sums[pl.ds(me * own_blocks, own_blocks)]
    for d, copy in enumerate(point_copies):
        copy.wait_recv()
        total = total + point_in[d]
    points = point_update(total, own[...])
    if last:
        for k in range(3):
            new_points[:, k, :] = points[k]
        window_copies = []
    else:
        here_points = pl.ds(me * own_blocks, own_blocks)
        new_points[here_points] = own[...]
        for k in range(3):
            new_points[here_points, k, :] = points[k]
        window_copies = [
            send(3, d, peer, new_points.at[here_points], new_points.at[here_points])
            for d, peer in enumerate(peers)
        ]

    for copy in frame_copies + point_copies:
        copy.wait_send()
    for copy in pose_copies + window_copies:
        copy.wait()

    @pl.when(row < rows - 1)
    def _():
        edge(0, row + 1).wait_send()

    @pl.when(row > 0)
    def _():
        edge(1, row - 1).wait_send()


def exchange(frame_sums, point_sums, state, own, count, rows, last):
    frame_blocks = state.shape[0]
    own_blocks = own.shape[0]
    share = frame_blocks // count
    vmem = pl.BlockSpec(memory_space=pltpu.VMEM)
    point_blocks = own_blocks if last else own_blocks * count
    return pl.pallas_call(
        functools.partial(exchange_kernel, count, rows, last),
        out_shape=[
            jax.ShapeDtypeStruct(state.shape, jnp.float32),
            jax.ShapeDtypeStruct((point_blocks,) + own.shape[1:], jnp.float32),
        ],
        in_specs=[vmem] * 4,
        out_specs=[vmem] * 2,
        scratch_shapes=[
            pltpu.VMEM((count - 1, share, 16, 128), jnp.float32),
            pltpu.VMEM((count - 1, own_blocks, 8, 128), jnp.float32),
            pltpu.VMEM((2, 16, TILE), jnp.float32),
            pltpu.VMEM((frame_blocks + 2, 16, TILE), jnp.float32),
            pltpu.SemaphoreType.DMA((4, count - 1)),
            pltpu.SemaphoreType.DMA((4, count - 1)),
            pltpu.SemaphoreType.DMA((2,)),
            pltpu.SemaphoreType.DMA((2,)),
        ],
        compiler_params=pltpu.CompilerParams(
            collective_id=2 if last else 1, has_side_effects=True
        ),
        name="exchange_last" if last else "exchange_first",
    )(frame_sums, point_sums, state, own)


def on_device(
    camera_poses,
    landmarks,
    odometry,
    odometry_info,
    observations,
    tile_frame,
    tile_block,
    tile_count,
    block_slot,
):
    frames = camera_poses.shape[1]
    blocks = frames // TILE
    rows, count = lax.axis_size("tm"), lax.axis_size("lm")
    own_blocks = landmarks.shape[1] // TILE
    packed = jnp.concatenate(
        [camera_poses, odometry, odometry_info[None, :], jnp.zeros((3, frames), jnp.float32)],
        axis=0,
    )
    state = jnp.transpose(packed.reshape(16, blocks, TILE), (1, 0, 2))
    own = jnp.concatenate([landmarks, jnp.zeros((5, own_blocks * TILE), jnp.float32)], axis=0)
    own = jnp.transpose(own.reshape(8, own_blocks, TILE), (1, 0, 2))
    window = gather_points(own, count)
    for iteration in range(ITERS):
        last = iteration == ITERS - 1
        frame_sums, point_sums = tile_sums(
            state, window, observations, tile_frame, tile_block, tile_count, block_slot
        )
        state, window = exchange(frame_sums, point_sums, state, own, count, rows, last)
        if not last:
            own = lax.dynamic_slice_in_dim(
                window, lax.axis_index("lm") * own_blocks, own_blocks, 0
            )
    poses = jnp.transpose(state[:, 0:6, :], (1, 0, 2)).reshape(6, frames)
    points = jnp.transpose(window[:, 0:3, :], (1, 0, 2)).reshape(3, own_blocks * TILE)
    return (poses, points)


def solution(mesh):
    return jax.shard_map(
        on_device,
        mesh=mesh,
        in_specs=(
            P(None, "tm"),
            P(None, ("tm", "lm")),
            P(None, "tm"),
            P("tm"),
            P(("tm", "lm"), None, None, None),
            P(("tm", "lm")),
            P(("tm", "lm")),
            P(("tm", "lm")),
            P("tm", None),
        ),
        out_specs=(P(None, "tm"), P(None, ("tm", "lm"))),
        check_vma=False,
    )
```

time: 179 us -> 122 us (0.68)
  Pallas kernels: 0 us -> 96 us
  waiting for transfers between devices: 54.8 us -> 0 us
  other arithmetic: 41.1 us -> 0.08 us
  blocking collectives: 22.2 us -> 0 us
  between operations: 15.6 us -> 1.48 us
  starting transfers between devices: 9.93 us -> 0 us
  local copies, waits for them, and re-layouts: 31.7 us -> 24.5 us
  matrix products: 2.62 us -> 0 us
    pallas_call x0 -> x5, Pallas kernels: none -> 96 us  [the longest x2 50.6 us: tile_sums(): pl.pallas_call(tiles_kernel, grid_spec=grid_spec, out_shape=[jax.ShapeDty...]
    reduce_scatter x4 -> x0, waiting for transfers between devices: 48.3 us -> none  [the longest x2 29.8 us: on_device(): lax.psum_scatter(frame_local, 'lm', scatter_dimension=1, tiled=True)]
    reduce_sum x5 -> x0, other arithmetic: 23.2 us -> none  [the longest x2 14.7 us: tile_terms(): jnp.sum(weight * (rotation_rows[a] * rotation_rows[b]), axis=1)]
    all_gather x4 -> x0, blocking collectives: 22.2 us -> none  [the longest x2 11.8 us: fetch_window(): return lax.all_gather(owned_points, 'lm', axis=1, tiled=True)]
    mul x35 -> x0, local copies, waits for them, and re-layouts: 19.4 us -> none  [the longest x12 7.8 us: tile_terms(): point_columns[a] * point_columns[b]]
    unnamed x103 -> x35, local copies, waits for them, and re-layouts: 1.01 us -> 19 us
    ppermute x4 -> x0, starting transfers between devices: 9.77 us -> none  [the longest x2 7.18 us: extended_2(): before = lax.ppermute(last, axis, up)]
    mul x14 -> x0, other arithmetic: 8.43 us -> none  [the longest x2 3.74 us: tile_terms(): weighted = [weight * residual[k] for k in range(3)]]
  transfers between devices with their start and end apart: 8 -> 0, of which waited for: 6 -> 0; matrix products, arithmetic and copies ran while one was open for 5% -> 0% of each run, Pallas kernels for 0% -> 0%
where the time goes in v1:
time: 122 us
  Pallas kernels  96 us (79%)
  local copies, waits for them, and re-layouts  24.5 us (20%)
  between operations  1.48 us (1%)
    pallas_call x2, Pallas kernels, tile_sums(): pl.pallas_call(tiles_kernel, grid_spec=grid_spec, out_shape=[jax.ShapeDty...  50.6 us
    pallas_call x2, Pallas kernels, exchange(): pl.pallas_call(functools.partial(exchange_kernel, count, rows, last), out...  38.6 us
    unnamed x35, local copies, waits for them, and re-layouts  19 us
    pallas_call x1, Pallas kernels, gather_points(): pl.pallas_call(functools.partial(gather_kernel, count), out_shape=jax.Sha...  6.69 us

profile of v1, /device:TPU:0, one launch (start us, length us, event | category | flops | bytes accessed | tf_op | source)
XLA Modules:
  0.0 122.0 jit_solution(940624721578151201)
XLA Ops:
  0.7 8.9 %copy.16.obs = bf16[96,3,64,64]{3,2,1,0:T(8,128)(2,1)} copy(bf16[96,3,64,64]{0,3,2,1:T(8,128)(2,1)} %param.13) | data formatting | bytes 4718592 | tf_op args[4]
  9.8 0.1 concatenate.15
  9.9 0.1 pad.4.clone
  10.0 0.1 maximum_bitcast_fusion.poses.state
  10.2 0.6 copy.21
  10.8 6.7 %gather_points.1.window = f32[32,8,64]{2,1,0:T(8,128)} custom-call(f32[8,8,64]{2,1,0:T(8,128)} %bitcast.9), custom_call_target="tpu_custom_call" | custom-call | tf_op jit(solution)/shard_map/gather_points/pallas_call | solution.py:317
  18.2 2.3 %copy-done = bf16[96,3,64,64]{3,2,1,0:T(8,128)(2,1)S(1)} copy-done((bf16[96,3,64,64]{3,2,1,0:T(8,128)(2,1)S(1)}, bf16[96,3,64,64]{3,2,1,0:T(8,128)(2,1)}, u32[]{:S(2)}) %copy-start) | copy-done | bytes 2359320
  20.5 0.9 copy-done.3
  21.4 25.3 %tile_sums.2 = (f32[16,16,128]{2,1,0:T(8,128)S(1)}, f32[32,8,128]{2,1,0:T(8,128)S(1)}) custom-call(s32[96]{0:T(128)S(1)} %copy-done.10, s32[96]{0:T(128)S(1)} %copy-done.11, s32[1]{0:T(128)S(6)} %copy.22.tile_count, s32[1,32]{1,0:T(1,128)S(1)} %copy-done.12, f32[16,16,64]{2,1,0:T(8,128)S(1)} %maximum_bitcast_fusion.poses.state, f32[32,8,64]{2,1,0:T(8,128)S(1)} %copy-done.3, ...), custom_call_target="tpu_custom_call" | custom-call | tf_op jit(solution)/shard_map/tile_sums/pallas_call | solution.py:253
  46.7 0.7 copy-done.8
  47.4 0.7 copy-done.9
  48.1 21.0 %exchange_first.1 = (f32[16,16,64]{2,1,0:T(8,128)}, f32[32,8,64]{2,1,0:T(8,128)}) custom-call(f32[16,16,128]{2,1,0:T(8,128)} %copy-done.8, f32[32,8,128]{2,1,0:T(8,128)} %copy-done.9, f32[16,16,64]{2,1,0:T(8,128)} %copy-done.2, f32[8,8,64]{2,1,0:T(8,128)} %bitcast.10), custom_call_target="tpu_custom_call" | custom-call | tf_op jit(solution)/shard_map/exchange_first/pallas_call | solution.py:566
  69.1 2.3 %copy-done.1 = bf16[96,3,64,64]{3,2,1,0:T(8,128)(2,1)S(1)} copy-done((bf16[96,3,64,64]{3,2,1,0:T(8,128)(2,1)S(1)}, bf16[96,3,64,64]{3,2,1,0:T(8,128)(2,1)}, u32[]{:S(2)}) %copy-start.1) | copy-done | bytes 2359320
  71.4 0.9 copy-done.4
  72.3 0.9 copy-done.5
  73.2 25.3 %tile_sums.3 = (f32[16,16,128]{2,1,0:T(8,128)S(1)}, f32[32,8,128]{2,1,0:T(8,128)S(1)}) custom-call(s32[96]{0:T(128)S(1)} %copy-done.10, s32[96]{0:T(128)S(1)} %copy-done.11, s32[1]{0:T(128)S(6)} %copy.22.tile_count, s32[1,32]{1,0:T(1,128)S(1)} %copy-done.12, f32[16,16,64]{2,1,0:T(8,128)S(1)} %copy-done.4, f32[32,8,64]{2,1,0:T(8,128)S(1)} %copy-done.5, ...), custom_call_target="tpu_custom_call" | custom-call | tf_op jit(solution)/shard_map/tile_sums/pallas_call | solution.py:253
  98.6 0.7 copy-done.6
  99.3 0.7 copy-done.7
  99.9 1.4 %constant_dynamic-slice_fusion.own = f32[8,8,64]{2,1,0:T(8,128)} fusion(f32[32,8,64]{2,1,0:T(8,128)} %get-tuple-element.13.window, s32[]{:T(128)S(6)} %select_n.3), kind=kLoop, calls=%fused_computation.4 | loop fusion | bytes 32772 | tf_op jit(solution)/shard_map/dynamic_slice | solution.py:621
  101.3 17.7 %exchange_last.1 = (f32[16,16,64]{2,1,0:T(8,128)}, f32[8,8,64]{2,1,0:T(8,128)}) custom-call(f32[16,16,128]{2,1,0:T(8,128)} %copy-done.6, f32[32,8,128]{2,1,0:T(8,128)} %copy-done.7, f32[16,16,64]{2,1,0:T(8,128)} %get-tuple-element.12.poses.state, f32[8,8,64]{2,1,0:T(8,128)} %constant_dynamic-slice_fusion.own), custom_call_target="tpu_custom_call" | custom-call | tf_op jit(solution)/shard_map/exchange_last/pallas_call | solution.py:566
  119.0 0.8 slice_bitcast_fusion
  119.9 0.7 reshape.20
  120.5 0.8 slice_bitcast_fusion.1
  121.3 0.7 reshape.21
  (34 shorter events, 0.4 us)
Async XLA Ops:
  0.6 9.0 %copy-start.13 = (f32[6,1024]{1,0:T(8,128)S(1)}, f32[6,1024]{1,0:T(8,128)}, u32[]{:S(2)}) copy-start(f32[6,1024]{1,0:T(8,128)} %param.9) | copy-start | bytes 73732
  0.6 9.0 %copy-start.14 = (f32[6,1024]{1,0:T(8,128)S(1)}, f32[6,1024]{1,0:T(8,128)}, u32[]{:S(2)}) copy-start(f32[6,1024]{1,0:T(8,128)} %param.11) | copy-start | bytes 73732
  0.7 9.1 %copy-start.16 = (f32[1024]{0:T(1024)S(1)}, f32[1024]{0:T(1024)}, u32[]{:S(2)}) copy-start(f32[1024]{0:T(1024)} %param.12) | copy-start | bytes 12292
  0.7 9.4 %copy-start.15 = (f32[3,512]{1,0:T(4,128)S(1)}, f32[3,512]{1,0:T(4,128)}, u32[]{:S(2)}) copy-start(f32[3,512]{1,0:T(4,128)} %param.10) | copy-start | bytes 18436
  0.7 17.5 %copy-start.10 = (s32[96]{0:T(128)S(1)}, s32[96]{0:T(128)}, u32[]{:S(2)}) copy-start(s32[96]{0:T(128)} %tile_frame.3) | copy-start | bytes 1156
  0.7 17.5 %copy-start.11 = (s32[96]{0:T(128)S(1)}, s32[96]{0:T(128)}, u32[]{:S(2)}) copy-start(s32[96]{0:T(128)} %tile_block.3) | copy-start | bytes 1156
  0.7 17.5 %copy-start.12 = (s32[1,32]{1,0:T(1,128)S(1)}, s32[1,32]{1,0:T(1,128)}, u32[]{:S(2)}) copy-start(s32[1,32]{1,0:T(1,128)} %block_slot.3) | copy-start | bytes 388
  10.1 38.0 %copy-start.2 = (f32[16,16,64]{2,1,0:T(8,128)}, f32[16,16,64]{2,1,0:T(8,128)S(1)}, u32[]{:S(2)}) copy-start(f32[16,16,64]{2,1,0:T(8,128)S(1)} %maximum_bitcast_fusion.poses.state) | copy-start | bytes 196612
  18.2 2.3 %copy-start = (bf16[96,3,64,64]{3,2,1,0:T(8,128)(2,1)S(1)}, bf16[96,3,64,64]{3,2,1,0:T(8,128)(2,1)}, u32[]{:S(2)}) copy-start(bf16[96,3,64,64]{3,2,1,0:T(8,128)(2,1)} %copy.16.obs) | copy-start | bytes 7077892
  20.5 0.9 copy-start.3
  46.7 0.7 copy-start.8
  47.4 0.7 copy-start.9
  69.1 2.3 %copy-start.1 = (bf16[96,3,64,64]{3,2,1,0:T(8,128)(2,1)S(1)}, bf16[96,3,64,64]{3,2,1,0:T(8,128)(2,1)}, u32[]{:S(2)}) copy-start(bf16[96,3,64,64]{3,2,1,0:T(8,128)(2,1)} %copy.16.obs) | copy-start | bytes 7077892
  71.4 0.9 copy-start.4
  72.3 0.9 copy-start.5
  98.6 0.7 copy-start.6
  99.3 0.7 copy-start.7

commit v2 on v1

--- a/solution.py
+++ b/solution.py
@@ -60,7 +60,42 @@
     return high, low
 
 
+def repack_kernel(obs, packed):
+    part = pl.program_id(0)
+    slots = obs.shape[3]
+    images = packed.shape[0] // slots
+    row = lax.broadcasted_iota(jnp.int32, (slots, slots), 0)
+    column = lax.broadcasted_iota(jnp.int32, (slots, slots), 1)
+    identity = jnp.where(row == column, 1.0, 0.0).astype(jnp.bfloat16)
+
+    @pl.loop(0, HALF, step=4)
+    def _(start):
+        for u in range(4):
+            i = start + u
+            pairs = jnp.concatenate([obs[0, i], obs[0, i + HALF]], axis=0)
+            turned = lax.dot_general(
+                identity, pairs, (((1,), (1,)), ((), ())), preferred_element_type=jnp.float32
+            )
+            packed[pl.ds(part * HALF + i, slots, stride=images), :] = turned
+
+
+def repack(observations):
+    slots = observations.shape[0]
+    by_tile = jnp.transpose(observations, (1, 2, 3, 0))
+    packed = pl.pallas_call(
+        repack_kernel,
+        grid=(3,),
+        in_specs=[pl.BlockSpec((1, TILE, TILE, slots), lambda s: (s, 0, 0, 0))],
+        out_specs=pl.BlockSpec((slots * 3 * HALF, 128), lambda s: (0, 0)),
+        out_shape=jax.ShapeDtypeStruct((slots * 3 * HALF, 128), jnp.float32),
+        compiler_params=pltpu.CompilerParams(vmem_limit_bytes=48 * 1024 * 1024),
+        name="repack",
+    )(by_tile)
+    return packed.reshape(slots, 3 * HALF, 128)
+
+
 def tiles_kernel(
+    unroll,
     tile_frame,
     tile_block,
     tile_count,
@@ -160,12 +195,10 @@
             point_feat[block, 32:64, :] = low
 
     def one_tile(t, slot):
-        f = tile_frame[slot]
-        p = block_slot[0, tile_block[slot]]
-        measured = obs[t]
-        measured = jnp.concatenate(
-            [measured[:, :HALF, :], measured[:, HALF:, :]], axis=2
-        ).astype(jnp.float32)
+        live = slot < tile_count[0]
+        f = jnp.where(live, tile_frame[slot], 0)
+        p = jnp.where(live, block_slot[0, tile_block[slot]], 0)
+        measured = [obs[t, k * HALF : (k + 1) * HALF, :] for k in range(3)]
         x = [point_wide[p, k : k + 1, :] for k in range(3)]
         w = [pose_wide[f, k] for k in range(3)]
         turned = cross_product(w, x)
@@ -175,33 +208,34 @@
         squared = (
             residual[0] * residual[0] + residual[1] * residual[1] + residual[2] * residual[2]
         )
-        weight = 1.0 / (1.0 + squared * (1.0 / robust_scale))
+        weight = jnp.where(live, 1.0, 0.0) / (1.0 + squared * (1.0 / robust_scale))
         images = jnp.concatenate(
             [weight] + [weight * measured[k] for k in range(3)], axis=0
         )
         high, low = split_rows(images)
-        g = frame_feat[f]
-        with_high = lax.dot_general(
-            g, high, (((1,), (0,)), ((), ())), preferred_element_type=jnp.float32
-        )
-        with_low = lax.dot_general(
-            g[0:32], low, (((1,), (0,)), ((), ())), preferred_element_type=jnp.float32
-        )
-        point_acc[p] += with_high[0:32] + with_high[32:64] + with_low
-        h = point_feat[p]
-        with_high = lax.dot_general(
-            h, high, (((1,), (1,)), ((), ())), preferred_element_type=jnp.float32
-        )
-        with_low = lax.dot_general(
-            h[0:32], low, (((1,), (1,)), ((), ())), preferred_element_type=jnp.float32
-        )
-        frame_acc[f] += with_high[0:32] + with_high[32:64] + with_low
+        sums = []
+        for features, dims in ((frame_feat[f], (1, 0)), (point_feat[p], (1, 1))):
+            dims = (((dims[0],), (dims[1],)), ((), ()))
+            with_high = lax.dot_general(
+                features, high, dims, preferred_element_type=jnp.float32
+            )
+            with_low = lax.dot_general(
+                features[0:32], low, dims, preferred_element_type=jnp.float32
+            )
+            sums.append(with_high[0:32] + with_high[32:64] + with_low)
+        return f, p, sums
 
     here = jnp.clip(tile_count[0] - step * step_tiles, 0, step_tiles)
 
-    @pl.loop(0, here)
-    def _(t):
-        one_tile(t, step * step_tiles + t)
+    @pl.loop(0, (here + unroll - 1) // unroll)
+    def _(group):
+        done = []
+        for u in range(unroll):
+            t = group * unroll + u
+            done.append(one_tile(t, step * step_tiles + t))
+        for f, p, sums in done:
+            point_acc[p] += sums[0]
+            frame_acc[f] += sums[1]
 
     @pl.when(step == pl.num_programs(0) - 1)
     def _():
@@ -226,9 +260,8 @@
 def tile_sums(poses, window, observations, tile_frame, tile_block, tile_count, block_slot):
     slots = observations.shape[0]
     frame_blocks, point_blocks = poses.shape[0], window.shape[0]
-    steps = 4
-    while slots % steps:
-        steps -= 1
+    steps = 2 if slots % 2 == 0 else 1
+    unroll = max(u for u in (1, 2, 3, 4) if slots // steps % u == 0)
     whole = lambda shape: pl.BlockSpec(shape, lambda s, *_: (0,) * len(shape))
     grid_spec = pltpu.PrefetchScalarGridSpec(
         num_scalar_prefetch=4,
@@ -236,7 +269,7 @@
         in_specs=[
             whole(poses.shape),
             whole(window.shape),
-            pl.BlockSpec((slots // steps, 3, TILE, TILE), lambda s, *_: (s, 0, 0, 0)),
+            pl.BlockSpec((slots // steps, 3 * HALF, 128), lambda s, *_: (s, 0, 0)),
         ],
         out_specs=[whole((frame_blocks, 16, 128)), whole((point_blocks, 8, 128))],
         scratch_shapes=[
@@ -251,7 +284,7 @@
         ],
     )
     return pl.pallas_call(
-        tiles_kernel,
+        functools.partial(tiles_kernel, unroll),
         grid_spec=grid_spec,
         out_shape=[
             jax.ShapeDtypeStruct((frame_blocks, 16, 128), jnp.float32),
@@ -426,7 +459,8 @@
     state,
     own,
     new_state,
-    new_points,
+    new_own,
+    new_window,
     frame_in,
     point_in,
     edge_in,
@@ -529,19 +563,19 @@
         copy.wait_recv()
         total = total + point_in[d]
     points = point_update(total, own[...])
+    new_own[...] = own[...]
+    for k in range(3):
+        new_own[:, k, :] = points[k]
+    window_copies = []
     if last:
-        for k in range(3):
-            new_points[:, k, :] = points[k]
-        window_copies = []
+        new_window[...] = jnp.zeros_like(new_window)
     else:
         here_points = pl.ds(me * own_blocks, own_blocks)
-        new_points[here_points] = own[...]
-        for k in range(3):
-            new_points[here_points, k, :] = points[k]
         window_copies = [
-            send(3, d, peer, new_points.at[here_points], new_points.at[here_points])
+            send(3, d, peer, new_own, new_window.at[here_points])
             for d, peer in enumerate(peers)
         ]
+        new_window[here_points] = new_own[...]
 
     for copy in frame_copies + point_copies:
         copy.wait_send()
@@ -562,15 +596,16 @@
     own_blocks = own.shape[0]
     share = frame_blocks // count
     vmem = pl.BlockSpec(memory_space=pltpu.VMEM)
-    point_blocks = own_blocks if last else own_blocks * count
+    point_blocks = 1 if last else own_blocks * count
     return pl.pallas_call(
         functools.partial(exchange_kernel, count, rows, last),
         out_shape=[
             jax.ShapeDtypeStruct(state.shape, jnp.float32),
+            jax.ShapeDtypeStruct(own.shape, jnp.float32),
             jax.ShapeDtypeStruct((point_blocks,) + own.shape[1:], jnp.float32),
         ],
         in_specs=[vmem] * 4,
-        out_specs=[vmem] * 2,
+        out_specs=[vmem] * 3,
         scratch_shapes=[
             pltpu.VMEM((count - 1, share, 16, 128), jnp.float32),
             pltpu.VMEM((count - 1, own_blocks, 8, 128), jnp.float32),
@@ -610,19 +645,16 @@
     state = jnp.transpose(packed.reshape(16, blocks, TILE), (1, 0, 2))
     own = jnp.concatenate([landmarks, jnp.zeros((5, own_blocks * TILE), jnp.float32)], axis=0)
     own = jnp.transpose(own.reshape(8, own_blocks, TILE), (1, 0, 2))
+    observations = repack(observations)
     window = gather_points(own, count)
     for iteration in range(ITERS):
         last = iteration == ITERS - 1
         frame_sums, point_sums = tile_sums(
             state, window, observations, tile_frame, tile_block, tile_count, block_slot
         )
-        state, window = exchange(frame_sums, point_sums, state, own, count, rows, last)
-        if not last:
-            own = lax.dynamic_slice_in_dim(
-                window, lax.axis_index("lm") * own_blocks, own_blocks, 0
-            )
+        state, own, window = exchange(frame_sums, point_sums, state, own, count, rows, last)
     poses = jnp.transpose(state[:, 0:6, :], (1, 0, 2)).reshape(6, frames)
-    points = jnp.transpose(window[:, 0:3, :], (1, 0, 2)).reshape(3, own_blocks * TILE)
+    points = jnp.transpose(own[:, 0:3, :], (1, 0, 2)).reshape(3, own_blocks * TILE)
     return (poses, points)
 
 

time: 122 us -> 90.5 us (0.74)
  Pallas kernels: 96 us -> 69.7 us
  local copies, waits for them, and re-layouts: 24.5 us -> 18 us
    pallas_call x2 -> x3, Pallas kernels: 50.6 us -> 34.3 us  [the longest x2 25.3 us: tile_sums(): pl.pallas_call(functools.partial(tiles_kernel, unroll), grid_spec=grid_sp...]
    pallas_call x2, Pallas kernels: 38.6 us -> 28.7 us  [exchange(): pl.pallas_call(functools.partial(exchange_kernel, count, rows, last), out...]
    unnamed x35 -> x28, local copies, waits for them, and re-layouts: 19 us -> 11.1 us
    concatenate x6, local copies, waits for them, and re-layouts: 0.35 us -> 2.55 us  [on_device(): jnp.concatenate([camera_poses, odometry, odometry_info[None, :], jnp.zero...]
    dynamic_slice x1 -> x0, local copies, waits for them, and re-layouts: 1.37 us -> none  [on_device(): lax.dynamic_slice_in_dim(window, lax.axis_index('lm') * own_blocks, own_b...]
where the time goes in v2:
time: 90.5 us; the launch traced here: 89.3 us
  Pallas kernels  69.7 us (77%)
  local copies, waits for them, and re-layouts  18 us (20%)
  between operations  1.42 us (2%)
    pallas_call x2, Pallas kernels, exchange(): pl.pallas_call(functools.partial(exchange_kernel, count, rows, last), out...  28.7 us
    pallas_call x2, Pallas kernels, tile_sums(): pl.pallas_call(functools.partial(tiles_kernel, unroll), grid_spec=grid_sp...  25.3 us
    unnamed x28, local copies, waits for them, and re-layouts  11.1 us
    pallas_call x1, Pallas kernels, repack(): pl.pallas_call(repack_kernel, grid=(3,), in_specs=[pl.BlockSpec((1, TILE,...  8.99 us
    pallas_call x1, Pallas kernels, gather_points(): pl.pallas_call(functools.partial(gather_kernel, count), out_shape=jax.Sha...  6.73 us
    concatenate x6, local copies, waits for them, and re-layouts, on_device(): jnp.concatenate([camera_poses, odometry, odometry_info[None, :], jnp.zero...  2.55 us

profile of v2, /device:TPU:0, one launch (start us, length us, event | category | flops | bytes accessed | tf_op | source)
XLA Modules:
  0.0 89.3 jit_solution(12932824950671096678)
XLA Ops:
  1.4 0.8 concatenate.15
  2.2 0.7 concatenate.17
  3.0 0.6 copy.17
  3.6 0.8 concatenate.13
  4.4 0.8 concatenate.14
  5.4 6.7 %gather_points.1.window = f32[32,8,64]{2,1,0:T(8,128)} custom-call(f32[8,8,64]{2,1,0:T(8,128)} %bitcast.14), custom_call_target="tpu_custom_call" | custom-call | tf_op jit(solution)/shard_map/gather_points/pallas_call | solution.py:350
  12.1 1.9 %copy-done.2 = bf16[96,3,64,64]{0,3,2,1:T(8,128)(2,1)S(1)} copy-done((bf16[96,3,64,64]{0,3,2,1:T(8,128)(2,1)S(1)}, bf16[96,3,64,64]{0,3,2,1:T(8,128)(2,1)}, u32[]{:S(2)}) %copy-start.2) | copy-done | bytes 2359320
  14.0 9.0 %repack.1 = f32[9216,128]{1,0:T(8,128)} custom-call(bf16[3,64,64,96]{3,2,1,0:T(8,128)(2,1)S(1)} %bitcast.13), custom_call_target="tpu_custom_call" | custom-call | tf_op jit(solution)/shard_map/repack/pallas_call | solution.py:85
  23.0 2.3 %copy-done = f32[9216,128]{1,0:T(8,128)S(1)} copy-done((f32[9216,128]{1,0:T(8,128)S(1)}, f32[9216,128]{1,0:T(8,128)}, u32[]{:S(2)}) %copy-start) | copy-done | bytes 4718616
  25.4 12.7 %tile_sums.2 = (f32[16,16,128]{2,1,0:T(8,128)S(1)}, f32[32,8,128]{2,1,0:T(8,128)S(1)}) custom-call(s32[96]{0:T(128)S(1)} %copy-done.11, s32[96]{0:T(128)S(1)} %copy-done.12, s32[1]{0:T(128)S(6)} %copy.18.tile_count, s32[1,32]{1,0:T(1,128)S(1)} %copy-done.13, f32[16,16,64]{2,1,0:T(8,128)S(1)} %maximum_bitcast_fusion.poses.state, f32[32,8,64]{2,1,0:T(8,128)S(1)} %copy-done.4, ...), custom_call_target="tpu_custom_call" | custom-call | tf_op jit(solution)/shard_map/tile_sums/pallas_call | solution.py:286
  38.0 0.7 copy-done.9
  38.7 0.7 copy-done.10
  39.4 15.9 %exchange_first.1 = (f32[16,16,64]{2,1,0:T(8,128)}, f32[8,8,64]{2,1,0:T(8,128)}, f32[32,8,64]{2,1,0:T(8,128)}) custom-call(f32[16,16,128]{2,1,0:T(8,128)} %copy-done.9, f32[32,8,128]{2,1,0:T(8,128)} %copy-done.10, f32[16,16,64]{2,1,0:T(8,128)} %copy-done.3, f32[8,8,64]{2,1,0:T(8,128)} %bitcast.15), custom_call_target="tpu_custom_call" | custom-call | tf_op jit(solution)/shard_map/exchange_first/pallas_call | solution.py:600
  55.3 2.3 %copy-done.1 = f32[9216,128]{1,0:T(8,128)S(1)} copy-done((f32[9216,128]{1,0:T(8,128)S(1)}, f32[9216,128]{1,0:T(8,128)}, u32[]{:S(2)}) %copy-start.1) | copy-done | bytes 4718616
  57.6 0.9 %copy-done.5 = f32[16,16,64]{2,1,0:T(8,128)S(1)} copy-done((f32[16,16,64]{2,1,0:T(8,128)S(1)}, f32[16,16,64]{2,1,0:T(8,128)}, u32[]{:S(2)}) %copy-start.5) | copy-done | bytes 65560
  58.6 0.9 %copy-done.6 = f32[32,8,64]{2,1,0:T(8,128)S(1)} copy-done((f32[32,8,64]{2,1,0:T(8,128)S(1)}, f32[32,8,64]{2,1,0:T(8,128)}, u32[]{:S(2)}) %copy-start.6) | copy-done | bytes 65560
  59.5 12.7 %tile_sums.3 = (f32[16,16,128]{2,1,0:T(8,128)S(1)}, f32[32,8,128]{2,1,0:T(8,128)S(1)}) custom-call(s32[96]{0:T(128)S(1)} %copy-done.11, s32[96]{0:T(128)S(1)} %copy-done.12, s32[1]{0:T(128)S(6)} %copy.18.tile_count, s32[1,32]{1,0:T(1,128)S(1)} %copy-done.13, f32[16,16,64]{2,1,0:T(8,128)S(1)} %copy-done.5, f32[32,8,64]{2,1,0:T(8,128)S(1)} %copy-done.6, ...), custom_call_target="tpu_custom_call" | custom-call | tf_op jit(solution)/shard_map/tile_sums/pallas_call | solution.py:286
  72.1 0.7 copy-done.7
  72.8 0.6 copy-done.8
  73.5 12.8 %exchange_last.1 = (f32[16,16,64]{2,1,0:T(8,128)}, f32[8,8,64]{2,1,0:T(8,128)}, f32[1,8,64]{2,1,0:T(8,128)}) custom-call(f32[16,16,128]{2,1,0:T(8,128)} %copy-done.7, f32[32,8,128]{2,1,0:T(8,128)} %copy-done.8, f32[16,16,64]{2,1,0:T(8,128)} %get-tuple-element.13.poses.state, f32[8,8,64]{2,1,0:T(8,128)} %get-tuple-element.17.own), custom_call_target="tpu_custom_call" | custom-call | tf_op jit(solution)/shard_map/exchange_last/pallas_call | solution.py:600
  86.3 0.8 slice_bitcast_fusion
  87.1 0.7 reshape.24
  87.8 0.8 slice_bitcast_fusion.1
  88.6 0.7 reshape.25
  (27 shorter events, 0.3 us)
Async XLA Ops:
  0.6 22.4 %copy-start.13 = (s32[1,32]{1,0:T(1,128)S(1)}, s32[1,32]{1,0:T(1,128)}, u32[]{:S(2)}) copy-start(s32[1,32]{1,0:T(1,128)} %block_slot.3) | copy-start | bytes 388
  0.6 22.4 %copy-start.12 = (s32[96]{0:T(128)S(1)}, s32[96]{0:T(128)}, u32[]{:S(2)}) copy-start(s32[96]{0:T(128)} %tile_block.3) | copy-start | bytes 1156
  0.7 22.4 %copy-start.11 = (s32[96]{0:T(128)S(1)}, s32[96]{0:T(128)}, u32[]{:S(2)}) copy-start(s32[96]{0:T(128)} %tile_frame.3) | copy-start | bytes 1156
  5.4 32.7 %copy-start.3 = (f32[16,16,64]{2,1,0:T(8,128)}, f32[16,16,64]{2,1,0:T(8,128)S(1)}, u32[]{:S(2)}) copy-start(f32[16,16,64]{2,1,0:T(8,128)S(1)} %maximum_bitcast_fusion.poses.state) | copy-start | bytes 196612
  12.1 1.9 %copy-start.2 = (bf16[96,3,64,64]{0,3,2,1:T(8,128)(2,1)S(1)}, bf16[96,3,64,64]{0,3,2,1:T(8,128)(2,1)}, u32[]{:S(2)}) copy-start(bf16[96,3,64,64]{0,3,2,1:T(8,128)(2,1)} %param.13) | copy-start | bytes 7077892
  14.0 9.0 %copy-start.4 = (f32[32,8,64]{2,1,0:T(8,128)S(1)}, f32[32,8,64]{2,1,0:T(8,128)}, u32[]{:S(2)}) copy-start(f32[32,8,64]{2,1,0:T(8,128)} %gather_points.1.window) | copy-start | bytes 196612
  23.0 2.3 %copy-start = (f32[9216,128]{1,0:T(8,128)S(1)}, f32[9216,128]{1,0:T(8,128)}, u32[]{:S(2)}) copy-start(f32[9216,128]{1,0:T(8,128)} %repack.1) | copy-start | bytes 14155780
  38.0 0.7 copy-start.9
  38.7 0.7 copy-start.10
  55.3 2.3 %copy-start.1 = (f32[9216,128]{1,0:T(8,128)S(1)}, f32[9216,128]{1,0:T(8,128)}, u32[]{:S(2)}) copy-start(f32[9216,128]{1,0:T(8,128)} %repack.1) | copy-start | bytes 14155780
  57.6 0.9 %copy-start.5 = (f32[16,16,64]{2,1,0:T(8,128)S(1)}, f32[16,16,64]{2,1,0:T(8,128)}, u32[]{:S(2)}) copy-start(f32[16,16,64]{2,1,0:T(8,128)} %get-tuple-element.13.poses.state) | copy-start | bytes 196612
  58.6 0.9 %copy-start.6 = (f32[32,8,64]{2,1,0:T(8,128)S(1)}, f32[32,8,64]{2,1,0:T(8,128)}, u32[]{:S(2)}) copy-start(f32[32,8,64]{2,1,0:T(8,128)} %get-tuple-element.14.window) | copy-start | bytes 196612
  72.1 0.7 copy-start.7
  72.8 0.6 copy-start.8

commit v3 on v2

v3 whole, which is shorter than its diff:
```python
import functools

import jax
import jax.numpy as jnp
from jax import lax
from jax.experimental import pallas as pl
from jax.experimental.pallas import tpu as pltpu
from jax.sharding import PartitionSpec as P

TILE = 64
HALF = 32
ITERS = 2
VMEM_LIMIT = 60 * 1024 * 1024
MESH = pl.DeviceIdType.MESH

robust_scale = 4.0
damping = 1.0
moment_pairs = ((0, 0), (1, 1), (2, 2), (0, 1), (0, 2), (1, 2))


def cross_product(left, right):
    return [
        left[1] * right[2] - left[2] * right[1],
        left[2] * right[0] - left[0] * right[2],
        left[0] * right[1] - left[1] * right[0],
    ]


def block_solve(matrix, vector):
    dimension = len(vector)
    factor = [[None] * dimension for i in range(dimension)]
    inverse_diag = [None] * dimension
    for i in range(dimension):
        for j in range(i + 1):
            running = matrix[i][j]
            for k in range(j):
                running = running - factor[i][k] * factor[j][k]
            if i == j:
                factor[i][i] = jnp.sqrt(running)
                inverse_diag[i] = 1.0 / factor[i][i]
            else:
                factor[i][j] = running * inverse_diag[j]
    forward = [None] * dimension
    for i in range(dimension):
        running = vector[i]
        for k in range(i):
            running = running - factor[i][k] * forward[k]
        forward[i] = running * inverse_diag[i]
    solution = [None] * dimension
    for i in reversed(range(dimension)):
        running = forward[i]
        for k in range(i + 1, dimension):
            running = running - factor[k][i] * solution[k]
        solution[i] = running * inverse_diag[i]
    return solution


def split_rows(value):
    high = value.astype(jnp.bfloat16)
    low = (value - high.astype(jnp.float32)).astype(jnp.bfloat16)
    return high, low


def pick_rows(rows, sub, default=0.0):
    value = jnp.full(sub.shape, default, jnp.float32)
    for s, row in rows.items():
        value = jnp.where(sub == s, row, value)
    return value


def frame_features(block_poses, sub, lane):
    image = lane // HALF
    first = image == 0
    features, linear = [], {}
    for half in range(2):
        part = block_poses[:, half * HALF : (half + 1) * HALF]
        part = jnp.concatenate([part] * 4, axis=1)
        value = [jnp.broadcast_to(part[k : k + 1], (8, 128)) for k in range(6)]
        w, t = value[0:3], value[3:6]
        turned = cross_product(w, t)
        rows = {}
        for m in range(3):
            a, b = (m + 1) % 3, (m + 2) % 3
            row = jnp.where(first, t[m] - turned[m], 0.0)
            row = jnp.where(image == 1 + m, -1.0, row)
            row = jnp.where(image == 1 + b, w[a], row)
            rows[m] = jnp.where(image == 1 + a, -w[b], row)
        square = w[0] * w[0] + w[1] * w[1] + w[2] * w[2]
        rows[3] = jnp.where(first, 1.0 + square, 0.0)
        products = [jnp.where(first, w[a] * w[b], 0.0) for a, b in moment_pairs]
        for m in range(4):
            rows[4 + m] = products[m]
        features.append(pick_rows(rows, sub))
        features.append(pick_rows({0: products[4], 1: products[5]}, sub))
        second, third = image == 1, image == 2
        zero = jnp.zeros_like(w[0])

        def by_part(x, y, z):
            return jnp.where(first, x, jnp.where(second, y, jnp.where(third, z, zero)))

        linear[half * 4] = by_part(t[0], t[1], t[2])
        linear[half * 4 + 1] = by_part(1.0, w[2], -w[1])
        linear[half * 4 + 2] = by_part(-w[2], 1.0, w[0])
        linear[half * 4 + 3] = by_part(w[1], -w[0], 1.0)
    return features, pick_rows(linear, sub)


def point_features(block_points, sub, lane):
    upper = lane >= TILE
    both = jnp.concatenate([block_points, block_points], axis=1)
    x = [jnp.broadcast_to(both[k : k + 1], (8, 128)) for k in range(3)]
    low = pick_rows({1: x[0], 2: x[1], 3: x[2]}, sub, 1.0)
    high = pick_rows({5: x[0], 6: x[1], 7: x[2]}, sub, 1.0)
    low = jnp.where((sub < 4) & jnp.logical_not(upper), low, 0.0)
    high = jnp.where((sub >= 4) & upper, high, 0.0)
    left = pick_rows({m: x[a] for m, (a, b) in enumerate(moment_pairs)}, sub)
    right = pick_rows({m: x[b] for m, (a, b) in enumerate(moment_pairs)}, sub)
    moments = left * right
    return [
        low,
        jnp.where(upper, 0.0, moments),
        high,
        jnp.where(upper, moments, 0.0),
    ]


def tiles_kernel(
    chunks,
    unroll,
    tile_frame,
    tile_block,
    tile_count,
    block_slot,
    poses_far,
    window_far,
    obs_far,
    frame_out,
    point_out,
    poses,
    window,
    obs,
    frame_feat,
    point_feat,
    frame_line,
    point_line,
    frame_acc,
    point_acc,
    sems,
):
    frame_blocks = poses.shape[0]
    point_blocks = window.shape[0]
    chunk_rows = obs.shape[1] // chunks
    chunk_tiles = chunk_rows // HALF

    def chunk_copy(c):
        part = pl.ds(c * chunk_rows, chunk_rows)
        return pltpu.make_async_copy(obs_far.at[:, part], obs.at[:, part], sems.at[2 + c])

    window_copy = pltpu.make_async_copy(window_far, window, sems.at[0])
    pose_copy = pltpu.make_async_copy(poses_far, poses, sems.at[1])
    window_copy.start()
    pose_copy.start()
    for c in range(chunks):
        chunk_copy(c).start()
    frame_acc[...] = jnp.zeros_like(frame_acc)
    point_acc[...] = jnp.zeros_like(point_acc)
    sub = lax.broadcasted_iota(jnp.int32, (8, 128), 0)
    lane = lax.broadcasted_iota(jnp.int32, (8, 128), 1)
    zeros = jnp.zeros((8, 128), jnp.float32)

    window_copy.wait()

    @pl.loop(0, point_blocks, step=4)
    def _(start):
        for u in range(4):
            block = start + u
            rows = point_features(window[block], sub, lane)
            high, low = split_rows(jnp.concatenate(rows, axis=0))
            point_feat[block, 0:32, :] = high
            point_feat[block, 32:64, :] = low
            ones = rows[0] + rows[2]
            high = ones.astype(jnp.bfloat16).astype(jnp.float32)
            stack = jnp.concatenate([high, ones - high, high, zeros], axis=0)
            point_line[block] = stack.astype(jnp.bfloat16)

    pose_copy.wait()

    @pl.loop(0, frame_blocks, step=2)
    def _(start):
        for u in range(2):
            block = start + u
            rows, linear = frame_features(poses[block, 0:8, :], sub, lane)
            high, low = split_rows(jnp.concatenate(rows, axis=0))
            frame_feat[block, 0:32, :] = high
            frame_feat[block, 32:64, :] = low
            high = linear.astype(jnp.bfloat16).astype(jnp.float32)
            stack = jnp.concatenate([high, high, linear - high, zeros], axis=0)
            frame_line[block] = jnp.transpose(stack)[0:96].astype(jnp.bfloat16)

    def one_tile(slot):
        live = slot < tile_count[0]
        f = jnp.where(live, tile_frame[slot], 0)
        p = jnp.where(live, block_slot[0, tile_block[slot]], 0)
        here = pl.ds(pl.multiple_of(slot * HALF, HALF), HALF)
        measured = [obs[k, here, :] for k in range(3)]
        seen = jnp.dot(frame_line[f], point_line[p], preferred_element_type=jnp.float32)
        residual = [seen[k * HALF : (k + 1) * HALF] - measured[k] for k in range(3)]
        squared = (
            residual[0] * residual[0] + residual[1] * residual[1] + residual[2] * residual[2]
        )
        weight = jnp.where(live, 1.0, 0.0) / (1.0 + squared * (1.0 / robust_scale))
        images = jnp.concatenate(
            [weight] + [weight * measured[k] for k in range(3)], axis=0
        )
        high, low = split_rows(images)
        sums = []
        for features, dims in ((frame_feat[f], (1, 0)), (point_feat[p], (1, 1))):
            dims = (((dims[0],), (dims[1],)), ((), ()))
            with_high = lax.dot_general(
                features, high, dims, preferred_element_type=jnp.float32
            )
            with_low = lax.dot_general(
                features[0:32], low, dims, preferred_element_type=jnp.float32
            )
            sums.append(with_high[0:32] + with_high[32:64] + with_low)
        return f, p, sums

    for c in range(chunks):
        chunk_copy(c).wait()
        here = jnp.clip(tile_count[0] - c * chunk_tiles, 0, chunk_tiles)

        @pl.loop(0, (here + unroll - 1) // unroll)
        def _(group):
            done = []
            for u in range(unroll):
                done.append(one_tile(c * chunk_tiles + group * unroll + u))
            for f, p, sums in done:
                point_acc[p] += sums[0]
                frame_acc[f] += sums[1]

    for block in range(frame_blocks):
        total = frame_acc[block]
        frame_out[block, 0:8, :] = total[0:8] + total[16:24]
        frame_out[block, 8:16, :] = jnp.where(
            lane < HALF, total[8:16], pltpu.roll(total[24:32], HALF, 1)
        )

    @pl.loop(0, point_blocks, step=4)
    def _(start):
        for u in range(4):
            total = point_acc[start + u]
            point_out[start + u] = jnp.where(
                lane >= TILE,
                pltpu.roll(total[8:16], TILE, 1) + total[24:32],
                total[0:8] + pltpu.roll(total[16:24], TILE, 1),
            )


def tile_sums(poses, window, packed, tile_frame, tile_block, tile_count, block_slot):
    slots = packed.shape[1] // HALF
    frame_blocks, point_blocks = poses.shape[0], window.shape[0]
    chunks = 2 if slots % 2 == 0 else 1
    unroll = max(u for u in (1, 2, 3, 4) if slots // chunks % u == 0)
    smem = pl.BlockSpec(memory_space=pltpu.SMEM)
    far = pl.BlockSpec(memory_space=pl.ANY)
    vmem = pl.BlockSpec(memory_space=pltpu.VMEM)
    return pl.pallas_call(
        functools.partial(tiles_kernel, chunks, unroll),
        in_specs=[smem] * 4 + [far] * 3,
        out_specs=[vmem] * 2,
        scratch_shapes=[
            pltpu.VMEM(poses.shape, jnp.float32),
            pltpu.VMEM(window.shape, jnp.float32),
            pltpu.VMEM(packed.shape, jnp.float32),
            pltpu.VMEM((frame_blocks, 64, 128), jnp.bfloat16),
            pltpu.VMEM((point_blocks, 64, 128), jnp.bfloat16),
            pltpu.VMEM((frame_blocks, 96, 32), jnp.bfloat16),
            pltpu.VMEM((point_blocks, 32, 128), jnp.bfloat16),
            pltpu.VMEM((frame_blocks, 32, 128), jnp.float32),
            pltpu.VMEM((point_blocks, 32, 128), jnp.float32),
            pltpu.SemaphoreType.DMA((2 + chunks,)),
        ],
        out_shape=[
            jax.ShapeDtypeStruct((frame_blocks, 16, 128), jnp.float32),
            jax.ShapeDtypeStruct((point_blocks, 8, 128), jnp.float32),
        ],
        compiler_params=pltpu.CompilerParams(vmem_limit_bytes=VMEM_LIMIT),
        name="tile_sums",
    )(tile_frame, tile_block, tile_count, block_slot, poses, window, packed)


def ring_peers(count):
    me = lax.axis_index("lm")
    return me, [lax.rem(me + d, count) for d in range(1, count)]


def greet(peers, row, rows):
    barrier = pltpu.get_barrier_semaphore()
    for peer in peers:
        pl.semaphore_signal(barrier, inc=1, device_id=(row, peer), device_id_type=MESH)
    if rows is None:
        pl.semaphore_wait(barrier, len(peers))
        return
    me = lax.axis_index("lm")

    @pl.when(row > 0)
    def _():
        pl.semaphore_signal(barrier, inc=1, device_id=(row - 1, me), device_id_type=MESH)

    @pl.when(row < rows - 1)
    def _():
        pl.semaphore_signal(barrier, inc=1, device_id=(row + 1, me), device_id_type=MESH)

    edges = jnp.minimum(row, 1) + jnp.minimum(rows - 1 - row, 1)
    pl.semaphore_wait(barrier, len(peers) + edges)


def prepare_kernel(
    count,
    camera_poses,
    odometry,
    odometry_info,
    landmarks,
    obs_far,
    state,
    own,
    window,
    packed_far,
    obs,
    packed,
    send_sem,
    recv_sem,
    load_sem,
    store_sem,
):
    row = lax.axis_index("tm")
    me, peers = ring_peers(count)
    blocks = own.shape[0]
    frame_blocks = state.shape[0]
    slots = obs.shape[3]
    loads = [
        pltpu.make_async_copy(obs_far.at[k], obs.at[k], load_sem.at[k]) for k in range(3)
    ]
    for load in loads:
        load.start()
    own[...] = jnp.zeros_like(own)
    for block in range(blocks):
        own[block, 0:3, :] = landmarks[:, block * TILE : (block + 1) * TILE]
    greet(peers, row, None)
    copies = []
    for d, peer in enumerate(peers):
        copies.append(
            pltpu.make_async_remote_copy(
                src_ref=own,
                dst_ref=window.at[pl.ds(me * blocks, blocks)],
                send_sem=send_sem.at[d],
                recv_sem=recv_sem.at[d],
                device_id=(row, peer),
                device_id_type=MESH,
            )
        )
        copies[-1].start()
    window[pl.ds(me * blocks, blocks)] = own[...]
    state[...] = jnp.zeros_like(state)
    for block in range(frame_blocks):
        here = slice(block * TILE, (block + 1) * TILE)
        state[block, 0:6, :] = camera_poses[:, here]
        state[block, 6:12, :] = odometry[:, here]
        state[block, 12:13, :] = odometry_info[:, here]

    row_id = lax.broadcasted_iota(jnp.int32, (slots, slots), 0)
    column_id = lax.broadcasted_iota(jnp.int32, (slots, slots), 1)
    identity = jnp.where(row_id == column_id, 1.0, 0.0).astype(jnp.bfloat16)
    stores = []
    for k in range(3):
        loads[k].wait()

        @pl.loop(0, HALF, step=8)
        def _(start):
            for u in range(8):
                i = start + u
                pairs = jnp.concatenate([obs[k, i], obs[k, i + HALF]], axis=0)
                turned = lax.dot_general(
                    identity,
                    pairs,
                    (((1,), (1,)), ((), ())),
                    preferred_element_type=jnp.float32,
                )
                packed[k, pl.ds(i, slots, stride=HALF), :] = turned

        stores.append(
            pltpu.make_async_copy(packed.at[k], packed_far.at[k], store_sem.at[k])
        )
        stores[-1].start()
    for copy in copies + stores:
        copy.wait()


def prepare(camera_poses, odometry, odometry_info, landmarks, observations, count):
    slots = observations.shape[0]
    frame_blocks = camera_poses.shape[1] // TILE
    blocks = landmarks.shape[1] // TILE
    by_tile = jnp.transpose(observations, (1, 2, 3, 0))
    vmem = pl.BlockSpec(memory_space=pltpu.VMEM)
    far = pl.BlockSpec(memory_space=pl.ANY)
    packed_shape = (3, slots * HALF, 128)
    return pl.pallas_call(
        functools.partial(prepare_kernel, count),
        out_shape=[
            jax.ShapeDtypeStruct((frame_blocks, 16, TILE), jnp.float32),
            jax.ShapeDtypeStruct((blocks, 8, TILE), jnp.float32),
            jax.ShapeDtypeStruct((blocks * count, 8, TILE), jnp.float32),
            jax.ShapeDtypeStruct(packed_shape, jnp.float32),
        ],
        in_specs=[vmem] * 4 + [far],
        out_specs=[vmem] * 3 + [far],
        scratch_shapes=[
            pltpu.VMEM(by_tile.shape, jnp.bfloat16),
            pltpu.VMEM(packed_shape, jnp.float32),
            pltpu.SemaphoreType.DMA((count - 1,)),
            pltpu.SemaphoreType.DMA((count - 1,)),
            pltpu.SemaphoreType.DMA((3,)),
            pltpu.SemaphoreType.DMA((3,)),
        ],
        compiler_params=pltpu.CompilerParams(
            collective_id=0, has_side_effects=True, vmem_limit_bytes=VMEM_LIMIT
        ),
        name="prepare",
    )(camera_poses, odometry, odometry_info[None, :], landmarks, by_tile)


def pose_update(total, state, before, after, final):
    def both(row_low, row_high, start):
        return jnp.concatenate(
            [total[:, row_low, start : start + HALF], total[:, row_high, start : start + HALF]],
            axis=1,
        )

    counted = both(0, 4, 0)
    centroid = [both(1 + k, 5 + k, 0) for k in range(3)]
    moments = [total[:, 8 + m, 0:TILE] for m in range(6)]
    seen = [both(0, 4, HALF * (1 + k)) for k in range(3)]

    def lever(a, k):
        return both(1 + a, 5 + a, HALF * (1 + k))

    current = [state[:, k, :] for k in range(6)]
    w, t = current[0:3], current[3:6]
    turned = cross_product(w, centroid)
    grad_off = [centroid[k] + turned[k] + t[k] * counted - seen[k] for k in range(3)]
    matrix_rows = [
        [moments[0], moments[3], moments[4]],
        [moments[3], moments[1], moments[5]],
        [moments[4], moments[5], moments[2]],
    ]
    trace = moments[0] + moments[1] + moments[2]
    pushed = cross_product(centroid, t)
    grad_rot = []
    for k in range(3):
        a, b = (k + 1) % 3, (k + 2) % 3
        product = (
            matrix_rows[k][0] * w[0] + matrix_rows[k][1] * w[1] + matrix_rows[k][2] * w[2]
        )
        grad_rot.append(trace * w[k] - product + pushed[k] - (lever(a, b) - lever(b, a)))

    weight_before = before[:, 12, :]
    weight_after = jnp.where(final, 0.0, state[:, 12, :])
    link_grad = []
    for k in range(6):
        ahead = after[:, k, :] - current[k] - state[:, 6 + k, :]
        behind = current[k] - before[:, k, :] - before[:, 6 + k, :]
        link_grad.append(weight_before * behind - weight_after * ahead)
    diagonal_add = weight_after + weight_before + damping

    zero_entry = jnp.zeros_like(counted)
    rotation_block = [
        [moments[1] + moments[2] + diagonal_add, -moments[3], -moments[4]],
        [-moments[3], moments[0] + moments[2] + diagonal_add, -moments[5]],
        [-moments[4], -moments[5], moments[0] + moments[1] + diagonal_add],
    ]
    cross_block = [
        [zero_entry, -centroid[2], centroid[1]],
        [centroid[2], zero_entry, -centroid[0]],
        [-centroid[1], centroid[0], zero_entry],
    ]
    matrix = [rotation_block[i] + cross_block[i] for i in range(3)]
    for i in range(3):
        offset_row = [counted + diagonal_add if i == k else zero_entry for k in range(3)]
        matrix.append([cross_block[k][i] for k in range(3)] + offset_row)
    sums = grad_rot + grad_off
    step = block_solve(matrix, [sums[k] + link_grad[k] for k in range(6)])
    return [current[k] - step[k] for k in range(6)]


def point_update(total, own):
    x = [own[:, k, :] for k in range(3)]
    spread = total[:, 3, 0:TILE]
    outer = [total[:, 4 + m, 0:TILE] for m in range(4)]
    outer += [total[:, m, TILE:] for m in range(2)]
    rows = [
        [outer[0], outer[3], outer[4]],
        [outer[3], outer[1], outer[5]],
        [outer[4], outer[5], outer[2]],
    ]
    gradient = [
        total[:, k, 0:TILE]
        + spread * x[k]
        - (rows[k][0] * x[0] + rows[k][1] * x[1] + rows[k][2] * x[2])
        for k in range(3)
    ]
    diagonal = spread + damping
    matrix = [
        [diagonal - outer[0], -outer[3], -outer[4]],
        [-outer[3], diagonal - outer[1], -outer[5]],
        [-outer[4], -outer[5], diagonal - outer[2]],
    ]
    step = block_solve(matrix, gradient)
    return [x[k] - step[k] for k in range(3)]


def exchange_kernel(
    count,
    rows,
    last,
    frame_far,
    point_far,
    state_far,
    own_far,
    pose_out,
    own_out,
    window_out,
    frame_in,
    point_in,
    edge_in,
    extended,
    own,
    fresh,
    gathered,
    fresh_points,
    send_sem,
    recv_sem,
    edge_send,
    edge_recv,
    load_sem,
    store_sem,
):
    row = lax.axis_index("tm")
    me, peers = ring_peers(count)
    frame_blocks = state_far.shape[0]
    share = frame_blocks // count
    own_blocks = own_far.shape[0]
    here = pl.ds(me * share, share)
    here_points = pl.ds(me * own_blocks, own_blocks)
    greet(peers, row, rows)

    def send(group, d, peer, source, target):
        copy = pltpu.make_async_remote_copy(
            src_ref=source,
            dst_ref=target,
            send_sem=send_sem.at[group, d],
            recv_sem=recv_sem.at[group, d],
            device_id=(row, peer),
            device_id_type=MESH,
        )
        copy.start()
        return copy

    def edge(side, target_row):
        block = frame_blocks - 1 if side == 0 else 0
        return pltpu.make_async_remote_copy(
            src_ref=state_far.at[block],
            dst_ref=edge_in.at[side],
            send_sem=edge_send.at[side],
            recv_sem=edge_recv.at[side],
            device_id=(target_row, me),
            device_id_type=MESH,
        )

    frame_copies = [
        send(0, d, peer, frame_far.at[pl.ds(peer * share, share)], frame_in.at[d])
        for d, peer in enumerate(peers)
    ]

    @pl.when(row < rows - 1)
    def _():
        edge(0, row + 1).start()

    @pl.when(row > 0)
    def _():
        edge(1, row - 1).start()

    point_copies = [
        send(1, d, peer, point_far.at[pl.ds(peer * own_blocks, own_blocks)], point_in.at[d])
        for d, peer in enumerate(peers)
    ]
    loads = [
        pltpu.make_async_copy(source, target, load_sem.at[n])
        for n, (source, target) in enumerate(
            (
                (state_far, extended.at[pl.ds(1, frame_blocks)]),
                (frame_far.at[here], frame_in.at[count - 1]),
                (point_far.at[here_points], point_in.at[count - 1]),
                (own_far, own),
            )
        )
    ]
    for load in loads:
        load.start()
    extended[0] = jnp.zeros_like(extended[0])
    extended[frame_blocks + 1] = jnp.zeros_like(extended[0])
    for load in loads:
        load.wait()

    @pl.when(row > 0)
    def _():
        edge(0, row - 1).wait_recv()
        extended[0] = edge_in[0]

    @pl.when(row < rows - 1)
    def _():
        edge(1, row + 1).wait_recv()
        extended[frame_blocks + 1] = edge_in[1]

    first = me * share
    mine = extended[pl.ds(first + 1, share)]
    ahead = extended[pl.ds(first + 2, share)]
    behind = extended[pl.ds(first, share)]
    after = jnp.concatenate([mine[:, :, 1:], ahead[:, :, :1]], axis=2)
    before = jnp.concatenate([behind[:, :, TILE - 1 :], mine[:, :, : TILE - 1]], axis=2)
    block_index = lax.broadcasted_iota(jnp.int32, (share, TILE), 0) + first
    lane = lax.broadcasted_iota(jnp.int32, (share, TILE), 1)
    final = (block_index * TILE + lane) == jnp.where(
        row == rows - 1, frame_blocks * TILE - 1, -1
    )

    total = frame_in[count - 1]
    for d, copy in enumerate(frame_copies):
        copy.wait_recv()
        total = total + frame_in[d]
    poses = pose_update(total, mine, before, after, final)
    stores = []
    if last:
        gathered[here] = mine[:, 0:8, :]
        for k in range(6):
            gathered[here, k, :] = poses[k]
        pose_copies = [
            send(2, d, peer, gathered.at[here], gathered.at[here])
            for d, peer in enumerate(peers)
        ]
    else:
        fresh[...] = mine
        for k in range(6):
            fresh[:, k, :] = poses[k]
        pose_copies = [
            send(2, d, peer, fresh, pose_out.at[here]) for d, peer in enumerate(peers)
        ]
        stores.append(pltpu.make_async_copy(fresh, pose_out.at[here], store_sem.at[0]))
        stores[-1].start()

    total = point_in[count - 1]
    for d, copy in enumerate(point_copies):
        copy.wait_recv()
        total = total + point_in[d]
    points = point_update(total, own[...])
    window_copies = []
    fresh_points[...] = own[...]
    for k in range(3):
        fresh_points[:, k, :] = points[k]
    if last:
        for pair in range(own_blocks // 2):
            own_out[:, pair * 128 : (pair + 1) * 128] = jnp.concatenate(
                [fresh_points[2 * pair, 0:3, :], fresh_points[2 * pair + 1, 0:3, :]], axis=1
            )
        window_out[...] = jnp.zeros_like(window_out)
    else:
        window_copies = [
            send(3, d, peer, fresh_points, window_out.at[here_points])
            for d, peer in enumerate(peers)
        ]
        for n, target in enumerate((window_out.at[here_points], own_out)):
            stores.append(pltpu.make_async_copy(fresh_points, target, store_sem.at[1 + n]))
            stores[-1].start()

    for copy in frame_copies + point_copies:
        copy.wait_send()
    for copy in pose_copies + window_copies + stores:
        copy.wait()
    if last:
        for pair in range(frame_blocks // 2):
            pose_out[:, pair * 128 : (pair + 1) * 128] = jnp.concatenate(
                [gathered[2 * pair, 0:6, :], gathered[2 * pair + 1, 0:6, :]], axis=1
            )

    @pl.when(row < rows - 1)
    def _():
        edge(0, row + 1).wait_send()

    @pl.when(row > 0)
    def _():
        edge(1, row - 1).wait_send()


def exchange(frame_sums, point_sums, state, own, count, rows, last):
    frame_blocks = state.shape[0]
    own_blocks = own.shape[0]
    share = frame_blocks // count
    vmem = pl.BlockSpec(memory_space=pltpu.VMEM)
    far = pl.BlockSpec(memory_space=pl.ANY)
    if last:
        shapes = [(6, frame_blocks * TILE), (3, own_blocks * TILE), (8, 128)]
    else:
        shapes = [state.shape, own.shape, (own_blocks * count,) + own.shape[1:]]
    return pl.pallas_call(
        functools.partial(exchange_kernel, count, rows, last),
        out_shape=[jax.ShapeDtypeStruct(shape, jnp.float32) for shape in shapes],
        in_specs=[far] * 4,
        out_specs=[vmem if last else far] * 3,
        scratch_shapes=[
            pltpu.VMEM((count, share, 16, 128), jnp.float32),
            pltpu.VMEM((count, own_blocks, 8, 128), jnp.float32),
            pltpu.VMEM((2, 16, TILE), jnp.float32),
            pltpu.VMEM((frame_blocks + 2, 16, TILE), jnp.float32),
            pltpu.VMEM(own.shape, jnp.float32),
            pltpu.VMEM((share, 16, TILE), jnp.float32),
            pltpu.VMEM((frame_blocks, 8, TILE), jnp.float32),
            pltpu.VMEM(own.shape, jnp.float32),
            pltpu.SemaphoreType.DMA((4, count - 1)),
            pltpu.SemaphoreType.DMA((4, count - 1)),
            pltpu.SemaphoreType.DMA((2,)),
            pltpu.SemaphoreType.DMA((2,)),
            pltpu.SemaphoreType.DMA((4,)),
            pltpu.SemaphoreType.DMA((3,)),
        ],
        compiler_params=pltpu.CompilerParams(
            collective_id=2 if last else 1,
            has_side_effects=True,
            vmem_limit_bytes=VMEM_LIMIT,
        ),
        name="exchange_last" if last else "exchange_first",
    )(frame_sums, point_sums, state, own)


def on_device(
    camera_poses,
    landmarks,
    odometry,
    odometry_info,
    observations,
    tile_frame,
    tile_block,
    tile_count,
    block_slot,
):
    rows, count = lax.axis_size("tm"), lax.axis_size("lm")
    state, own, window, packed = prepare(
        camera_poses, odometry, odometry_info, landmarks, observations, count
    )
    for iteration in range(ITERS):
        frame_sums, point_sums = tile_sums(
            state, window, packed, tile_frame, tile_block, tile_count, block_slot
        )
        last = iteration == ITERS - 1
        state, own, window = exchange(frame_sums, point_sums, state, own, count, rows, last)
    return (state, own)


def solution(mesh):
    return jax.shard_map(
        on_device,
        mesh=mesh,
        in_specs=(
            P(None, "tm"),
            P(None, ("tm", "lm")),
            P(None, "tm"),
            P("tm"),
            P(("tm", "lm"), None, None, None),
            P(("tm", "lm")),
            P(("tm", "lm")),
            P(("tm", "lm")),
            P("tm", None),
        ),
        out_specs=(P(None, "tm"), P(None, ("tm", "lm"))),
        check_vma=False,
    )
```

time: 90.5 us -> 82.9 us (0.916)
  local copies, waits for them, and re-layouts: 18 us -> 2.67 us
  Pallas kernels: 69.7 us -> 78.5 us
    unnamed x28 -> x2, local copies, waits for them, and re-layouts: 11.1 us -> 2.67 us
    pallas_call x4 -> x3, Pallas kernels: 41.1 us -> 46 us  [the longest x2 34.5 us: tile_sums(): pl.pallas_call(functools.partial(tiles_kernel, chunks, unroll), in_specs=...]
    pallas_call x2, Pallas kernels: 28.7 us -> 32.5 us  [exchange(): pl.pallas_call(functools.partial(exchange_kernel, count, rows, last), out...]
    concatenate x7 -> x0, local copies, waits for them, and re-layouts: 3.25 us -> none  [the longest x6 2.55 us: on_device(): jnp.concatenate([camera_poses, odometry, odometry_info[None, :], jnp.zero...]
    reshape x4 -> x0, local copies, waits for them, and re-layouts: 2.07 us -> none  [the longest x2 0.7 us: on_device(): own = jnp.transpose(own.reshape(8, own_blocks, TILE), (1, 0, 2))]
    transpose x4 -> x0, local copies, waits for them, and re-layouts: 1.62 us -> none  [the longest x2 0.86 us: on_device(): poses = jnp.transpose(state[:, 0:6, :], (1, 0, 2)).reshape(6, frames)]
where the time goes in v3:
time: 82.9 us; the launch traced here: 82.5 us
  Pallas kernels  78.5 us (95%)
  local copies, waits for them, and re-layouts  2.67 us (3%)
  between operations  1.32 us (2%)
    pallas_call x2, Pallas kernels, tile_sums(): pl.pallas_call(functools.partial(tiles_kernel, chunks, unroll), in_specs=...  34.5 us
    pallas_call x2, Pallas kernels, exchange(): pl.pallas_call(functools.partial(exchange_kernel, count, rows, last), out...  32.5 us
    pallas_call x1, Pallas kernels, prepare(): pl.pallas_call(functools.partial(prepare_kernel, count), out_shape=[jax.S...  11.5 us
    unnamed x2, local copies, waits for them, and re-layouts  2.67 us

profile of v3, /device:TPU:0, one launch (start us, length us, event | category | flops | bytes accessed | tf_op | source)
XLA Modules:
  0.0 82.5 jit_solution(1869907644253095630)
XLA Ops:
  1.3 11.5 %prepare.1 = (f32[16,16,64]{2,1,0:T(8,128)}, f32[8,8,64]{2,1,0:T(8,128)}, f32[32,8,64]{2,1,0:T(8,128)}, f32[3,3072,128]{2,1,0:T(8,128)}) custom-call(f32[6,1024]{1,0:T(8,128)} %camera_poses.1, f32[6,1024]{1,0:T(8,128)} %odometry.1, f32[1,1024]{1,0:T(1,128)} %bitcast.3, f32[3,512]{1,0:T(4,128)} %landmarks.1, bf16[3,64,64,96]{3,2,1,0:T(8,128)(2,1)} %bitcast.2), custom_call_target="tpu_custom_call" | custom-call | tf_op jit(solution)/shard_map/prepare/pallas_call | solution.py:407
  12.7 17.2 %tile_sums.2 = (f32[16,16,128]{2,1,0:T(8,128)}, f32[32,8,128]{2,1,0:T(8,128)}) custom-call(s32[96]{0:T(128)} %tile_frame.3, s32[96]{0:T(128)} %tile_block.3, s32[1]{0:T(128)S(6)} %copy.13.tile_count, s32[1,32]{1,0:T(1,128)} %block_slot.3, f32[16,16,64]{2,1,0:T(8,128)} %get-tuple-element.15.poses_far.state_far, f32[32,8,64]{2,1,0:T(8,128)} %get-tuple-element.16.window_far, ...), custom_call_target="tpu_custom_call" | custom-call | tf_op jit(solution)/shard_map/tile_sums/pallas_call | solution.py:267
  30.0 16.5 %exchange_first.1 = (f32[16,16,64]{2,1,0:T(8,128)}, f32[8,8,64]{2,1,0:T(8,128)}, f32[32,8,64]{2,1,0:T(8,128)}) custom-call(f32[16,16,128]{2,1,0:T(8,128)} %get-tuple-element.18.frame_far, f32[32,8,128]{2,1,0:T(8,128)} %get-tuple-element.19.point_far, f32[16,16,64]{2,1,0:T(8,128)} %get-tuple-element.15.poses_far.state_far, f32[8,8,64]{2,1,0:T(8,128)} %get-tuple-element.20.own_far), custom_call_target="tpu_custom_call" | custom-call | tf_op jit(solution)/shard_map/exchange_first/pallas_call | solution.py:713
  46.5 17.3 %tile_sums.3 = (f32[16,16,128]{2,1,0:T(8,128)}, f32[32,8,128]{2,1,0:T(8,128)}) custom-call(s32[96]{0:T(128)} %tile_frame.3, s32[96]{0:T(128)} %tile_block.3, s32[1]{0:T(128)S(6)} %copy.13.tile_count, s32[1,32]{1,0:T(1,128)} %block_slot.3, f32[16,16,64]{2,1,0:T(8,128)} %get-tuple-element.21.poses_far.state_far, f32[32,8,64]{2,1,0:T(8,128)} %get-tuple-element.22.window_far, ...), custom_call_target="tpu_custom_call" | custom-call | tf_op jit(solution)/shard_map/tile_sums/pallas_call | solution.py:267
  63.8 16.0 %exchange_last.1 = (f32[6,1024]{1,0:T(8,128)}, f32[3,512]{1,0:T(4,128)}, f32[8,128]{1,0:T(8,128)}) custom-call(f32[16,16,128]{2,1,0:T(8,128)} %get-tuple-element.23.frame_far, f32[32,8,128]{2,1,0:T(8,128)} %get-tuple-element.24.point_far, f32[16,16,64]{2,1,0:T(8,128)} %get-tuple-element.21.poses_far.state_far, f32[8,8,64]{2,1,0:T(8,128)} %get-tuple-element.25.own_far), custom_call_target="tpu_custom_call" | custom-call | tf_op jit(solution)/shard_map/exchange_last/pallas_call | solution.py:713
  79.8 1.4 %copy.14 = f32[6,1024]{1,0:T(8,128)} copy(f32[6,1024]{1,0:T(8,128)} %get-tuple-element.30) | data formatting | bytes 49152
  81.2 1.3 %copy.15 = f32[3,512]{1,0:T(4,128)} copy(f32[3,512]{1,0:T(4,128)} %get-tuple-element.31) | data formatting | bytes 12288

commit v4 on v3

--- a/solution.py
+++ b/solution.py
@@ -71,7 +71,7 @@
 def frame_features(block_poses, sub, lane):
     image = lane // HALF
     first = image == 0
-    features, linear = [], {}
+    features = []
     for half in range(2):
         part = block_poses[:, half * HALF : (half + 1) * HALF]
         part = jnp.concatenate([part] * 4, axis=1)
@@ -92,17 +92,7 @@
             rows[4 + m] = products[m]
         features.append(pick_rows(rows, sub))
         features.append(pick_rows({0: products[4], 1: products[5]}, sub))
-        second, third = image == 1, image == 2
-        zero = jnp.zeros_like(w[0])
-
-        def by_part(x, y, z):
-            return jnp.where(first, x, jnp.where(second, y, jnp.where(third, z, zero)))
-
-        linear[half * 4] = by_part(t[0], t[1], t[2])
-        linear[half * 4 + 1] = by_part(1.0, w[2], -w[1])
-        linear[half * 4 + 2] = by_part(-w[2], 1.0, w[0])
-        linear[half * 4 + 3] = by_part(w[1], -w[0], 1.0)
-    return features, pick_rows(linear, sub)
+    return features
 
 
 def point_features(block_points, sub, lane):
@@ -141,8 +131,8 @@
     obs,
     frame_feat,
     point_feat,
-    frame_line,
-    point_line,
+    pose_wide,
+    point_wide,
     frame_acc,
     point_acc,
     sems,
@@ -166,7 +156,7 @@
     point_acc[...] = jnp.zeros_like(point_acc)
     sub = lax.broadcasted_iota(jnp.int32, (8, 128), 0)
     lane = lax.broadcasted_iota(jnp.int32, (8, 128), 1)
-    zeros = jnp.zeros((8, 128), jnp.float32)
+    wide_upper = lax.broadcasted_iota(jnp.int32, (HALF, 128), 1) >= TILE
 
     window_copy.wait()
 
@@ -178,10 +168,8 @@
             high, low = split_rows(jnp.concatenate(rows, axis=0))
             point_feat[block, 0:32, :] = high
             point_feat[block, 32:64, :] = low
-            ones = rows[0] + rows[2]
-            high = ones.astype(jnp.bfloat16).astype(jnp.float32)
-            stack = jnp.concatenate([high, ones - high, high, zeros], axis=0)
-            point_line[block] = stack.astype(jnp.bfloat16)
+            both = window[block]
+            point_wide[block] = jnp.concatenate([both, both], axis=1)
 
     pose_copy.wait()
 
@@ -189,13 +177,21 @@
     def _(start):
         for u in range(2):
             block = start + u
-            rows, linear = frame_features(poses[block, 0:8, :], sub, lane)
+            mine = poses[block, 0:8, :]
+            rows = frame_features(mine, sub, lane)
             high, low = split_rows(jnp.concatenate(rows, axis=0))
-            frame_feat[block, 0:32, :] = high
-            frame_feat[block, 32:64, :] = low
-            high = linear.astype(jnp.bfloat16).astype(jnp.float32)
-            stack = jnp.concatenate([high, high, linear - high, zeros], axis=0)
-            frame_line[block] = jnp.transpose(stack)[0:96].astype(jnp.bfloat16)
+            frame_feat[block, 0:32, 0:128] = high
+            frame_feat[block, 0:32, 128:256] = high
+            frame_feat[block, 32:64, 0:128] = low
+            frame_feat[block, 32:64, 128:256] = jnp.zeros_like(low)
+            columns = jnp.transpose(mine)
+            for k in range(6):
+                column = columns[:, k : k + 1]
+                pose_wide[block, k] = jnp.where(
+                    wide_upper,
+                    jnp.broadcast_to(column[HALF:], (HALF, 128)),
+                    jnp.broadcast_to(column[:HALF], (HALF, 128)),
+                )
 
     def one_tile(slot):
         live = slot < tile_count[0]
@@ -203,8 +199,12 @@
         p = jnp.where(live, block_slot[0, tile_block[slot]], 0)
         here = pl.ds(pl.multiple_of(slot * HALF, HALF), HALF)
         measured = [obs[k, here, :] for k in range(3)]
-        seen = jnp.dot(frame_line[f], point_line[p], preferred_element_type=jnp.float32)
-        residual = [seen[k * HALF : (k + 1) * HALF] - measured[k] for k in range(3)]
+        x = [point_wide[p, k : k + 1, :] for k in range(3)]
+        w = [pose_wide[f, k] for k in range(3)]
+        turned = cross_product(w, x)
+        residual = [
+            (x[k] + turned[k]) + (pose_wide[f, 3 + k] - measured[k]) for k in range(3)
+        ]
         squared = (
             residual[0] * residual[0] + residual[1] * residual[1] + residual[2] * residual[2]
         )
@@ -212,17 +212,17 @@
         images = jnp.concatenate(
             [weight] + [weight * measured[k] for k in range(3)], axis=0
         )
-        high, low = split_rows(images)
-        sums = []
-        for features, dims in ((frame_feat[f], (1, 0)), (point_feat[p], (1, 1))):
-            dims = (((dims[0],), (dims[1],)), ((), ()))
-            with_high = lax.dot_general(
-                features, high, dims, preferred_element_type=jnp.float32
-            )
-            with_low = lax.dot_general(
-                features[0:32], low, dims, preferred_element_type=jnp.float32
-            )
-            sums.append(with_high[0:32] + with_high[32:64] + with_low)
+        stacked = jnp.concatenate(split_rows(images), axis=0)
+        by_point = lax.dot_general(
+            frame_feat[f], stacked, (((1,), (0,)), ((), ())), preferred_element_type=jnp.float32
+        )
+        by_frame = lax.dot_general(
+            point_feat[p], stacked, (((1,), (1,)), ((), ())), preferred_element_type=jnp.float32
+        )
+        sums = (
+            by_point[0:32] + by_point[32:64],
+            by_frame[0:32, 0:128] + by_frame[0:32, 128:256] + by_frame[32:64, 0:128],
+        )
         return f, p, sums
 
     for c in range(chunks):
@@ -260,7 +260,7 @@
     slots = packed.shape[1] // HALF
     frame_blocks, point_blocks = poses.shape[0], window.shape[0]
     chunks = 2 if slots % 2 == 0 else 1
-    unroll = max(u for u in (1, 2, 3, 4) if slots // chunks % u == 0)
+    unroll = max(u for u in (1, 2, 3, 4, 6, 8) if slots // chunks % u == 0)
     smem = pl.BlockSpec(memory_space=pltpu.SMEM)
     far = pl.BlockSpec(memory_space=pl.ANY)
     vmem = pl.BlockSpec(memory_space=pltpu.VMEM)
@@ -272,10 +272,10 @@
             pltpu.VMEM(poses.shape, jnp.float32),
             pltpu.VMEM(window.shape, jnp.float32),
             pltpu.VMEM(packed.shape, jnp.float32),
-            pltpu.VMEM((frame_blocks, 64, 128), jnp.bfloat16),
+            pltpu.VMEM((frame_blocks, 64, 256), jnp.bfloat16),
             pltpu.VMEM((point_blocks, 64, 128), jnp.bfloat16),
-            pltpu.VMEM((frame_blocks, 96, 32), jnp.bfloat16),
-            pltpu.VMEM((point_blocks, 32, 128), jnp.bfloat16),
+            pltpu.VMEM((frame_blocks, 6, HALF, 128), jnp.float32),
+            pltpu.VMEM((point_blocks, 8, 128), jnp.float32),
             pltpu.VMEM((frame_blocks, 32, 128), jnp.float32),
             pltpu.VMEM((point_blocks, 32, 128), jnp.float32),
             pltpu.SemaphoreType.DMA((2 + chunks,)),
@@ -740,6 +740,30 @@
     )(frame_sums, point_sums, state, own)
 
 
+def emit_kernel(poses, points, poses_out, points_out, sems):
+    copies = [
+        pltpu.make_async_copy(poses, poses_out, sems.at[0]),
+        pltpu.make_async_copy(points, points_out, sems.at[1]),
+    ]
+    for copy in copies:
+        copy.start()
+    for copy in copies:
+        copy.wait()
+
+
+def emit(poses, points):
+    far = pl.BlockSpec(memory_space=pl.ANY)
+    return pl.pallas_call(
+        emit_kernel,
+        in_specs=[far] * 2,
+        out_specs=[far] * 2,
+        out_shape=[jax.ShapeDtypeStruct(a.shape, a.dtype) for a in (poses, points)],
+        scratch_shapes=[pltpu.SemaphoreType.DMA((2,))],
+        compiler_params=pltpu.CompilerParams(vmem_limit_bytes=VMEM_LIMIT),
+        name="emit",
+    )(poses, points)
+
+
 def on_device(
     camera_poses,
     landmarks,
@@ -761,7 +785,7 @@
         )
         last = iteration == ITERS - 1
         state, own, window = exchange(frame_sums, point_sums, state, own, count, rows, last)
-    return (state, own)
+    return tuple(emit(state, own))
 
 
 def solution(mesh):

time: 82.9 us -> 56.8 us (0.69)
  Pallas kernels: 78.5 us -> 55.4 us
  local copies, waits for them, and re-layouts: 2.67 us -> 0 us
    pallas_call x2, Pallas kernels: 34.5 us -> 18.5 us  [tile_sums(): pl.pallas_call(functools.partial(tiles_kernel, chunks, unroll), in_specs=...]
    pallas_call x2, Pallas kernels: 32.5 us -> 23.1 us  [exchange(): pl.pallas_call(functools.partial(exchange_kernel, count, rows, last), out...]
    unnamed x2 -> x0, local copies, waits for them, and re-layouts: 2.67 us -> none
    pallas_call x0 -> x1, Pallas kernels: none -> 2.36 us  [emit(): pl.pallas_call(emit_kernel, in_specs=[far] * 2, out_specs=[far] * 2, out_...]
where the time goes in v4:
time: 56.8 us
  Pallas kernels  55.4 us (98%)
  between operations  1.32 us (2%)
    pallas_call x2, Pallas kernels, exchange(): pl.pallas_call(functools.partial(exchange_kernel, count, rows, last), out...  23.1 us
    pallas_call x2, Pallas kernels, tile_sums(): pl.pallas_call(functools.partial(tiles_kernel, chunks, unroll), in_specs=...  18.5 us
    pallas_call x1, Pallas kernels, prepare(): pl.pallas_call(functools.partial(prepare_kernel, count), out_shape=[jax.S...  11.5 us
    pallas_call x1, Pallas kernels, emit(): pl.pallas_call(emit_kernel, in_specs=[far] * 2, out_specs=[far] * 2, out_...  2.36 us

profile of v4, /device:TPU:0, one launch (start us, length us, event | category | flops | bytes accessed | tf_op | source)
XLA Modules:
  0.0 56.8 jit_solution(2957804969020943098)
XLA Ops:
  1.3 11.5 %prepare.1 = (f32[16,16,64]{2,1,0:T(8,128)}, f32[8,8,64]{2,1,0:T(8,128)}, f32[32,8,64]{2,1,0:T(8,128)}, f32[3,3072,128]{2,1,0:T(8,128)}) custom-call(f32[6,1024]{1,0:T(8,128)} %camera_poses.1, f32[6,1024]{1,0:T(8,128)} %odometry.1, f32[1,1024]{1,0:T(1,128)} %bitcast.3, f32[3,512]{1,0:T(4,128)} %landmarks.1, bf16[3,64,64,96]{3,2,1,0:T(8,128)(2,1)} %bitcast.2), custom_call_target="tpu_custom_call" | custom-call | tf_op jit(solution)/shard_map/prepare/pallas_call | solution.py:407
  12.7 9.3 %tile_sums.2 = (f32[16,16,128]{2,1,0:T(8,128)}, f32[32,8,128]{2,1,0:T(8,128)}) custom-call(s32[96]{0:T(128)} %tile_frame.3, s32[96]{0:T(128)} %tile_block.3, s32[1]{0:T(128)S(6)} %copy.11.tile_count, s32[1,32]{1,0:T(1,128)} %block_slot.3, f32[16,16,64]{2,1,0:T(8,128)} %get-tuple-element.15.poses_far.state_far, f32[32,8,64]{2,1,0:T(8,128)} %get-tuple-element.16.window_far, ...), custom_call_target="tpu_custom_call" | custom-call | tf_op jit(solution)/shard_map/tile_sums/pallas_call | solution.py:267
  22.0 11.9 %exchange_first.1 = (f32[16,16,64]{2,1,0:T(8,128)}, f32[8,8,64]{2,1,0:T(8,128)}, f32[32,8,64]{2,1,0:T(8,128)}) custom-call(f32[16,16,128]{2,1,0:T(8,128)} %get-tuple-element.18.frame_far, f32[32,8,128]{2,1,0:T(8,128)} %get-tuple-element.19.point_far, f32[16,16,64]{2,1,0:T(8,128)} %get-tuple-element.15.poses_far.state_far, f32[8,8,64]{2,1,0:T(8,128)} %get-tuple-element.20.own_far), custom_call_target="tpu_custom_call" | custom-call | tf_op jit(solution)/shard_map/exchange_first/pallas_call | solution.py:713
  33.9 9.3 %tile_sums.3 = (f32[16,16,128]{2,1,0:T(8,128)}, f32[32,8,128]{2,1,0:T(8,128)}) custom-call(s32[96]{0:T(128)} %tile_frame.3, s32[96]{0:T(128)} %tile_block.3, s32[1]{0:T(128)S(6)} %copy.11.tile_count, s32[1,32]{1,0:T(1,128)} %block_slot.3, f32[16,16,64]{2,1,0:T(8,128)} %get-tuple-element.21.poses_far.state_far, f32[32,8,64]{2,1,0:T(8,128)} %get-tuple-element.22.window_far, ...), custom_call_target="tpu_custom_call" | custom-call | tf_op jit(solution)/shard_map/tile_sums/pallas_call | solution.py:267
  43.2 11.2 %exchange_last.1 = (f32[6,1024]{1,0:T(8,128)}, f32[3,512]{1,0:T(4,128)}, f32[8,128]{1,0:T(8,128)}) custom-call(f32[16,16,128]{2,1,0:T(8,128)} %get-tuple-element.23.frame_far, f32[32,8,128]{2,1,0:T(8,128)} %get-tuple-element.24.point_far, f32[16,16,64]{2,1,0:T(8,128)} %get-tuple-element.21.poses_far.state_far, f32[8,8,64]{2,1,0:T(8,128)} %get-tuple-element.25.own_far), custom_call_target="tpu_custom_call" | custom-call | tf_op jit(solution)/shard_map/exchange_last/pallas_call | solution.py:713
  54.4 2.4 %emit.1 = (f32[6,1024]{1,0:T(8,128)}, f32[3,512]{1,0:T(4,128)}) custom-call(f32[6,1024]{1,0:T(8,128)} %get-tuple-element.26.poses, f32[3,512]{1,0:T(4,128)} %get-tuple-element.27.points), custom_call_target="tpu_custom_call" | custom-call | tf_op jit(solution)/shard_map/emit/pallas_call | solution.py:756

commit v5 on v4

--- a/solution.py
+++ b/solution.py
@@ -97,8 +97,7 @@
 
 def point_features(block_points, sub, lane):
     upper = lane >= TILE
-    both = jnp.concatenate([block_points, block_points], axis=1)
-    x = [jnp.broadcast_to(both[k : k + 1], (8, 128)) for k in range(3)]
+    x = [jnp.broadcast_to(block_points[k], (8, 128)) for k in range(3)]
     low = pick_rows({1: x[0], 2: x[1], 3: x[2]}, sub, 1.0)
     high = pick_rows({5: x[0], 6: x[1], 7: x[2]}, sub, 1.0)
     low = jnp.where((sub < 4) & jnp.logical_not(upper), low, 0.0)
@@ -117,10 +116,10 @@
 def tiles_kernel(
     chunks,
     unroll,
-    tile_frame,
-    tile_block,
-    tile_count,
-    block_slot,
+    frame_list_far,
+    block_list_far,
+    count_far,
+    slot_far,
     poses_far,
     window_far,
     obs_far,
@@ -135,21 +134,38 @@
     point_wide,
     frame_acc,
     point_acc,
+    tile_frame,
+    tile_block,
+    tile_count,
+    block_slot,
     sems,
+    list_sems,
 ):
     frame_blocks = poses.shape[0]
     point_blocks = window.shape[0]
-    chunk_rows = obs.shape[1] // chunks
-    chunk_tiles = chunk_rows // HALF
+    chunk_tiles = obs.shape[1] // chunks
 
     def chunk_copy(c):
-        part = pl.ds(c * chunk_rows, chunk_rows)
+        part = pl.ds(c * chunk_tiles, chunk_tiles)
         return pltpu.make_async_copy(obs_far.at[:, part], obs.at[:, part], sems.at[2 + c])
 
     window_copy = pltpu.make_async_copy(window_far, window, sems.at[0])
     pose_copy = pltpu.make_async_copy(poses_far, poses, sems.at[1])
     window_copy.start()
     pose_copy.start()
+    lists = [
+        pltpu.make_async_copy(source, target, list_sems.at[n])
+        for n, (source, target) in enumerate(
+            (
+                (frame_list_far, tile_frame),
+                (block_list_far, tile_block),
+                (count_far, tile_count),
+                (slot_far, block_slot),
+            )
+        )
+    ]
+    for copy in lists:
+        copy.start()
     for c in range(chunks):
         chunk_copy(c).start()
     frame_acc[...] = jnp.zeros_like(frame_acc)
@@ -164,12 +180,16 @@
     def _(start):
         for u in range(4):
             block = start + u
-            rows = point_features(window[block], sub, lane)
+            line = window[pl.ds(block, 1), :]
+            both = []
+            for k in range(3):
+                part = line[:, k * TILE : (k + 1) * TILE]
+                both.append(jnp.concatenate([part, part], axis=1))
+                point_wide[block, k : k + 1, :] = both[k]
+            rows = point_features(both, sub, lane)
             high, low = split_rows(jnp.concatenate(rows, axis=0))
             point_feat[block, 0:32, :] = high
             point_feat[block, 32:64, :] = low
-            both = window[block]
-            point_wide[block] = jnp.concatenate([both, both], axis=1)
 
     pose_copy.wait()
 
@@ -197,8 +217,7 @@
         live = slot < tile_count[0]
         f = jnp.where(live, tile_frame[slot], 0)
         p = jnp.where(live, block_slot[0, tile_block[slot]], 0)
-        here = pl.ds(pl.multiple_of(slot * HALF, HALF), HALF)
-        measured = [obs[k, here, :] for k in range(3)]
+        measured = [obs[k, slot] for k in range(3)]
         x = [point_wide[p, k : k + 1, :] for k in range(3)]
         w = [pose_wide[f, k] for k in range(3)]
         turned = cross_product(w, x)
@@ -225,6 +244,8 @@
         )
         return f, p, sums
 
+    for copy in lists:
+        copy.wait()
     for c in range(chunks):
         chunk_copy(c).wait()
         here = jnp.clip(tile_count[0] - c * chunk_tiles, 0, chunk_tiles)
@@ -257,16 +278,15 @@
 
 
 def tile_sums(poses, window, packed, tile_frame, tile_block, tile_count, block_slot):
-    slots = packed.shape[1] // HALF
+    slots = packed.shape[1]
     frame_blocks, point_blocks = poses.shape[0], window.shape[0]
     chunks = 2 if slots % 2 == 0 else 1
     unroll = max(u for u in (1, 2, 3, 4, 6, 8) if slots // chunks % u == 0)
-    smem = pl.BlockSpec(memory_space=pltpu.SMEM)
     far = pl.BlockSpec(memory_space=pl.ANY)
     vmem = pl.BlockSpec(memory_space=pltpu.VMEM)
     return pl.pallas_call(
         functools.partial(tiles_kernel, chunks, unroll),
-        in_specs=[smem] * 4 + [far] * 3,
+        in_specs=[far] * 7,
         out_specs=[vmem] * 2,
         scratch_shapes=[
             pltpu.VMEM(poses.shape, jnp.float32),
@@ -278,7 +298,12 @@
             pltpu.VMEM((point_blocks, 8, 128), jnp.float32),
             pltpu.VMEM((frame_blocks, 32, 128), jnp.float32),
             pltpu.VMEM((point_blocks, 32, 128), jnp.float32),
+            pltpu.SMEM(tile_frame.shape, jnp.int32),
+            pltpu.SMEM(tile_block.shape, jnp.int32),
+            pltpu.SMEM(tile_count.shape, jnp.int32),
+            pltpu.SMEM(block_slot.shape, jnp.int32),
             pltpu.SemaphoreType.DMA((2 + chunks,)),
+            pltpu.SemaphoreType.DMA((4,)),
         ],
         out_shape=[
             jax.ShapeDtypeStruct((frame_blocks, 16, 128), jnp.float32),
@@ -323,6 +348,7 @@
     landmarks,
     obs_far,
     state,
+    links,
     own,
     window,
     packed_far,
@@ -343,16 +369,20 @@
     ]
     for load in loads:
         load.start()
+    own_rows = pl.ds(pl.multiple_of(me * blocks, blocks), blocks)
     own[...] = jnp.zeros_like(own)
     for block in range(blocks):
-        own[block, 0:3, :] = landmarks[:, block * TILE : (block + 1) * TILE]
+        for k in range(3):
+            own[block : block + 1, k * TILE : (k + 1) * TILE] = landmarks[
+                k : k + 1, block * TILE : (block + 1) * TILE
+            ]
     greet(peers, row, None)
     copies = []
     for d, peer in enumerate(peers):
         copies.append(
             pltpu.make_async_remote_copy(
                 src_ref=own,
-                dst_ref=window.at[pl.ds(me * blocks, blocks)],
+                dst_ref=window.at[own_rows],
                 send_sem=send_sem.at[d],
                 recv_sem=recv_sem.at[d],
                 device_id=(row, peer),
@@ -360,13 +390,14 @@
             )
         )
         copies[-1].start()
-    window[pl.ds(me * blocks, blocks)] = own[...]
+    window[own_rows] = own[...]
     state[...] = jnp.zeros_like(state)
+    links[...] = jnp.zeros_like(links)
     for block in range(frame_blocks):
         here = slice(block * TILE, (block + 1) * TILE)
         state[block, 0:6, :] = camera_poses[:, here]
-        state[block, 6:12, :] = odometry[:, here]
-        state[block, 12:13, :] = odometry_info[:, here]
+        links[block, 0:6, :] = odometry[:, here]
+        links[block, 6:7, :] = odometry_info[:, here]
 
     row_id = lax.broadcasted_iota(jnp.int32, (slots, slots), 0)
     column_id = lax.broadcasted_iota(jnp.int32, (slots, slots), 1)
@@ -377,16 +408,21 @@
 
         @pl.loop(0, HALF, step=8)
         def _(start):
+            turned = []
             for u in range(8):
-                i = start + u
-                pairs = jnp.concatenate([obs[k, i], obs[k, i + HALF]], axis=0)
-                turned = lax.dot_general(
-                    identity,
-                    pairs,
-                    (((1,), (1,)), ((), ())),
-                    preferred_element_type=jnp.float32,
+                pairs = jnp.concatenate(
+                    [obs[k, start + u], obs[k, start + u + HALF]], axis=0
                 )
-                packed[k, pl.ds(i, slots, stride=HALF), :] = turned
+                turned.append(
+                    lax.dot_general(
+                        identity,
+                        pairs,
+                        (((1,), (1,)), ((), ())),
+                        preferred_element_type=jnp.float32,
+                    )
+                )
+            here = pl.ds(pl.multiple_of(start, 8), 8)
+            packed[k, :, here, :] = jnp.swapaxes(jnp.stack(turned), 0, 1)
 
         stores.append(
             pltpu.make_async_copy(packed.at[k], packed_far.at[k], store_sem.at[k])
@@ -403,17 +439,18 @@
     by_tile = jnp.transpose(observations, (1, 2, 3, 0))
     vmem = pl.BlockSpec(memory_space=pltpu.VMEM)
     far = pl.BlockSpec(memory_space=pl.ANY)
-    packed_shape = (3, slots * HALF, 128)
+    packed_shape = (3, slots, HALF, 128)
     return pl.pallas_call(
         functools.partial(prepare_kernel, count),
         out_shape=[
-            jax.ShapeDtypeStruct((frame_blocks, 16, TILE), jnp.float32),
-            jax.ShapeDtypeStruct((blocks, 8, TILE), jnp.float32),
-            jax.ShapeDtypeStruct((blocks * count, 8, TILE), jnp.float32),
+            jax.ShapeDtypeStruct((frame_blocks, 8, TILE), jnp.float32),
+            jax.ShapeDtypeStruct((frame_blocks, 8, TILE), jnp.float32),
+            jax.ShapeDtypeStruct((blocks, 4 * TILE), jnp.float32),
+            jax.ShapeDtypeStruct((blocks * count, 4 * TILE), jnp.float32),
             jax.ShapeDtypeStruct(packed_shape, jnp.float32),
         ],
         in_specs=[vmem] * 4 + [far],
-        out_specs=[vmem] * 3 + [far],
+        out_specs=[vmem] * 4 + [far],
         scratch_shapes=[
             pltpu.VMEM(by_tile.shape, jnp.bfloat16),
             pltpu.VMEM(packed_shape, jnp.float32),
@@ -429,7 +466,7 @@
     )(camera_poses, odometry, odometry_info[None, :], landmarks, by_tile)
 
 
-def pose_update(total, state, before, after, final):
+def pose_update(total, state, links, before, links_before, after, final):
     def both(row_low, row_high, start):
         return jnp.concatenate(
             [total[:, row_low, start : start + HALF], total[:, row_high, start : start + HALF]],
@@ -463,12 +500,12 @@
         )
         grad_rot.append(trace * w[k] - product + pushed[k] - (lever(a, b) - lever(b, a)))
 
-    weight_before = before[:, 12, :]
-    weight_after = jnp.where(final, 0.0, state[:, 12, :])
+    weight_before = links_before[:, 6, :]
+    weight_after = jnp.where(final, 0.0, links[:, 6, :])
     link_grad = []
     for k in range(6):
-        ahead = after[:, k, :] - current[k] - state[:, 6 + k, :]
-        behind = current[k] - before[:, k, :] - before[:, 6 + k, :]
+        ahead = after[:, k, :] - current[k] - links[:, k, :]
+        behind = current[k] - before[:, k, :] - links_before[:, k, :]
         link_grad.append(weight_before * behind - weight_after * ahead)
     diagonal_add = weight_after + weight_before + damping
 
@@ -489,11 +526,11 @@
         matrix.append([cross_block[k][i] for k in range(3)] + offset_row)
     sums = grad_rot + grad_off
     step = block_solve(matrix, [sums[k] + link_grad[k] for k in range(6)])
-    return [current[k] - step[k] for k in range(6)]
+    return current, step
 
 
 def point_update(total, own):
-    x = [own[:, k, :] for k in range(3)]
+    x = [own[:, k * TILE : (k + 1) * TILE] for k in range(3)]
     spread = total[:, 3, 0:TILE]
     outer = [total[:, 4 + m, 0:TILE] for m in range(4)]
     outer += [total[:, m, TILE:] for m in range(2)]
@@ -515,42 +552,35 @@
         [-outer[4], -outer[5], diagonal - outer[2]],
     ]
     step = block_solve(matrix, gradient)
-    return [x[k] - step[k] for k in range(3)]
-
-
-def exchange_kernel(
-    count,
-    rows,
-    last,
-    frame_far,
-    point_far,
-    state_far,
-    own_far,
-    pose_out,
-    own_out,
-    window_out,
-    frame_in,
-    point_in,
-    edge_in,
-    extended,
-    own,
-    fresh,
-    gathered,
-    fresh_points,
-    send_sem,
-    recv_sem,
-    edge_send,
-    edge_recv,
-    load_sem,
-    store_sem,
-):
+    return x, step
+
+
+def exchange_kernel(count, rows, last, frame_far, point_far, state_far, links_far, own_far, *refs):
+    outs, refs = (refs[:4], refs[4:]) if last else (refs[:3], refs[3:])
+    (
+        frame_in,
+        point_in,
+        edge_in,
+        extended,
+        extended_links,
+        own,
+        fresh,
+        gathered,
+        fresh_points,
+        send_sem,
+        recv_sem,
+        edge_send,
+        edge_recv,
+        load_sem,
+        store_sem,
+    ) = refs
     row = lax.axis_index("tm")
     me, peers = ring_peers(count)
     frame_blocks = state_far.shape[0]
     share = frame_blocks // count
     own_blocks = own_far.shape[0]
     here = pl.ds(me * share, share)
-    here_points = pl.ds(me * own_blocks, own_blocks)
+    here_points = pl.ds(pl.multiple_of(me * own_blocks, own_blocks), own_blocks)
     greet(peers, row, rows)
 
     def send(group, d, peer, source, target):
@@ -566,9 +596,13 @@
         return copy
 
     def edge(side, target_row):
-        block = frame_blocks - 1 if side == 0 else 0
+        source = (
+            state_far.at[frame_blocks - 1],
+            links_far.at[frame_blocks - 1],
+            state_far.at[0],
+        )[side]
         return pltpu.make_async_remote_copy(
-            src_ref=state_far.at[block],
+            src_ref=source,
             dst_ref=edge_in.at[side],
             send_sem=edge_send.at[side],
             recv_sem=edge_recv.at[side],
@@ -584,10 +618,11 @@
     @pl.when(row < rows - 1)
     def _():
         edge(0, row + 1).start()
+        edge(1, row + 1).start()
 
     @pl.when(row > 0)
     def _():
-        edge(1, row - 1).start()
+        edge(2, row - 1).start()
 
     point_copies = [
         send(1, d, peer, point_far.at[pl.ds(peer * own_blocks, own_blocks)], point_in.at[d])
@@ -598,8 +633,9 @@
         for n, (source, target) in enumerate(
             (
                 (state_far, extended.at[pl.ds(1, frame_blocks)]),
+                (links_far, extended_links.at[pl.ds(1, frame_blocks)]),
                 (frame_far.at[here], frame_in.at[count - 1]),
-                (point_far.at[here_points], point_in.at[count - 1]),
+                (point_far.at[pl.ds(me * own_blocks, own_blocks)], point_in.at[count - 1]),
                 (own_far, own),
             )
         )
@@ -608,77 +644,93 @@
         load.start()
     extended[0] = jnp.zeros_like(extended[0])
     extended[frame_blocks + 1] = jnp.zeros_like(extended[0])
+    extended_links[0] = jnp.zeros_like(extended_links[0])
     for load in loads:
         load.wait()
+    if last:
+        for pair in range(frame_blocks // 2):
+            outs[0][:, pair * 128 : (pair + 1) * 128] = jnp.concatenate(
+                [extended[2 * pair + 1, 0:6, :], extended[2 * pair + 2, 0:6, :]], axis=1
+            )
 
     @pl.when(row > 0)
     def _():
         edge(0, row - 1).wait_recv()
+        edge(1, row - 1).wait_recv()
         extended[0] = edge_in[0]
+        extended_links[0] = edge_in[1]
 
     @pl.when(row < rows - 1)
     def _():
-        edge(1, row + 1).wait_recv()
-        extended[frame_blocks + 1] = edge_in[1]
+        edge(2, row + 1).wait_recv()
+        extended[frame_blocks + 1] = edge_in[2]
 
     first = me * share
+
+    def shifted(earlier, current):
+        return jnp.concatenate([earlier[:, :, TILE - 1 :], current[:, :, : TILE - 1]], axis=2)
+
     mine = extended[pl.ds(first + 1, share)]
+    mine_links = extended_links[pl.ds(first + 1, share)]
     ahead = extended[pl.ds(first + 2, share)]
-    behind = extended[pl.ds(first, share)]
     after = jnp.concatenate([mine[:, :, 1:], ahead[:, :, :1]], axis=2)
-    before = jnp.concatenate([behind[:, :, TILE - 1 :], mine[:, :, : TILE - 1]], axis=2)
+    before = shifted(extended[pl.ds(first, share)], mine)
+    links_before = shifted(extended_links[pl.ds(first, share)], mine_links)
     block_index = lax.broadcasted_iota(jnp.int32, (share, TILE), 0) + first
     lane = lax.broadcasted_iota(jnp.int32, (share, TILE), 1)
     final = (block_index * TILE + lane) == jnp.where(
         row == rows - 1, frame_blocks * TILE - 1, -1
     )
 
-    total = frame_in[count - 1]
-    for d, copy in enumerate(frame_copies):
+    for copy in frame_copies + point_copies:
         copy.wait_recv()
-        total = total + frame_in[d]
-    poses = pose_update(total, mine, before, after, final)
-    stores = []
+    frame_total, point_total = frame_in[count - 1], point_in[count - 1]
+    for d in range(count - 1):
+        frame_total = frame_total + frame_in[d]
+        point_total = point_total + point_in[d]
+    poses, pose_step = pose_update(
+        frame_total, mine, mine_links, before, links_before, after, final
+    )
+    points, point_step = point_update(point_total, own[...])
+    window_copies, stores = [], []
     if last:
-        gathered[here] = mine[:, 0:8, :]
+        gathered[here] = jnp.zeros_like(mine)
         for k in range(6):
-            gathered[here, k, :] = poses[k]
+            gathered[here, k, :] = pose_step[k]
         pose_copies = [
             send(2, d, peer, gathered.at[here], gathered.at[here])
             for d, peer in enumerate(peers)
         ]
+        for k in range(3):
+            for out, value in ((outs[2], points[k]), (outs[3], point_step[k])):
+                for pair in range(own_blocks // 2):
+                    out[k : k + 1, pair * 128 : (pair + 1) * 128] = jnp.concatenate(
+                        [value[2 * pair : 2 * pair + 1], value[2 * pair + 1 : 2 * pair + 2]],
+                        axis=1,
+                    )
     else:
+        pose_out, own_out, window_out = outs
         fresh[...] = mine
         for k in range(6):
-            fresh[:, k, :] = poses[k]
+            fresh[:, k, :] = poses[k] - pose_step[k]
         pose_copies = [
             send(2, d, peer, fresh, pose_out.at[here]) for d, peer in enumerate(peers)
         ]
-        stores.append(pltpu.make_async_copy(fresh, pose_out.at[here], store_sem.at[0]))
-        stores[-1].start()
-
-    total = point_in[count - 1]
-    for d, copy in enumerate(point_copies):
-        copy.wait_recv()
-        total = total + point_in[d]
-    points = point_update(total, own[...])
-    window_copies = []
-    fresh_points[...] = own[...]
-    for k in range(3):
-        fresh_points[:, k, :] = points[k]
-    if last:
-        for pair in range(own_blocks // 2):
-            own_out[:, pair * 128 : (pair + 1) * 128] = jnp.concatenate(
-                [fresh_points[2 * pair, 0:3, :], fresh_points[2 * pair + 1, 0:3, :]], axis=1
-            )
-        window_out[...] = jnp.zeros_like(window_out)
-    else:
+        fresh_points[...] = own[...]
+        for k in range(3):
+            fresh_points[:, k * TILE : (k + 1) * TILE] = points[k] - point_step[k]
         window_copies = [
             send(3, d, peer, fresh_points, window_out.at[here_points])
             for d, peer in enumerate(peers)
         ]
-        for n, target in enumerate((window_out.at[here_points], own_out)):
-            stores.append(pltpu.make_async_copy(fresh_points, target, store_sem.at[1 + n]))
+        for n, (source, target) in enumerate(
+            (
+                (fresh, pose_out.at[here]),
+                (fresh_points, window_out.at[here_points]),
+                (fresh_points, own_out),
+            )
+        ):
+            stores.append(pltpu.make_async_copy(source, target, store_sem.at[n]))
             stores[-1].start()
 
     for copy in frame_copies + point_copies:
@@ -687,48 +739,50 @@
         copy.wait()
     if last:
         for pair in range(frame_blocks // 2):
-            pose_out[:, pair * 128 : (pair + 1) * 128] = jnp.concatenate(
+            outs[1][:, pair * 128 : (pair + 1) * 128] = jnp.concatenate(
                 [gathered[2 * pair, 0:6, :], gathered[2 * pair + 1, 0:6, :]], axis=1
             )
 
     @pl.when(row < rows - 1)
     def _():
         edge(0, row + 1).wait_send()
+        edge(1, row + 1).wait_send()
 
     @pl.when(row > 0)
     def _():
-        edge(1, row - 1).wait_send()
-
-
-def exchange(frame_sums, point_sums, state, own, count, rows, last):
+        edge(2, row - 1).wait_send()
+
+
+def exchange(frame_sums, point_sums, state, links, own, count, rows, last):
     frame_blocks = state.shape[0]
     own_blocks = own.shape[0]
     share = frame_blocks // count
     vmem = pl.BlockSpec(memory_space=pltpu.VMEM)
     far = pl.BlockSpec(memory_space=pl.ANY)
     if last:
-        shapes = [(6, frame_blocks * TILE), (3, own_blocks * TILE), (8, 128)]
+        shapes = [(6, frame_blocks * TILE)] * 2 + [(3, own_blocks * TILE)] * 2
     else:
         shapes = [state.shape, own.shape, (own_blocks * count,) + own.shape[1:]]
     return pl.pallas_call(
         functools.partial(exchange_kernel, count, rows, last),
         out_shape=[jax.ShapeDtypeStruct(shape, jnp.float32) for shape in shapes],
-        in_specs=[far] * 4,
-        out_specs=[vmem if last else far] * 3,
+        in_specs=[far] * 5,
+        out_specs=[vmem if last else far] * len(shapes),
         scratch_shapes=[
             pltpu.VMEM((count, share, 16, 128), jnp.float32),
             pltpu.VMEM((count, own_blocks, 8, 128), jnp.float32),
-            pltpu.VMEM((2, 16, TILE), jnp.float32),
-            pltpu.VMEM((frame_blocks + 2, 16, TILE), jnp.float32),
+            pltpu.VMEM((3, 8, TILE), jnp.float32),
+            pltpu.VMEM((frame_blocks + 2, 8, TILE), jnp.float32),
+            pltpu.VMEM((frame_blocks + 2, 8, TILE), jnp.float32),
             pltpu.VMEM(own.shape, jnp.float32),
-            pltpu.VMEM((share, 16, TILE), jnp.float32),
+            pltpu.VMEM((share, 8, TILE), jnp.float32),
             pltpu.VMEM((frame_blocks, 8, TILE), jnp.float32),
             pltpu.VMEM(own.shape, jnp.float32),
             pltpu.SemaphoreType.DMA((4, count - 1)),
             pltpu.SemaphoreType.DMA((4, count - 1)),
-            pltpu.SemaphoreType.DMA((2,)),
-            pltpu.SemaphoreType.DMA((2,)),
-            pltpu.SemaphoreType.DMA((4,)),
+            pltpu.SemaphoreType.DMA((3,)),
+            pltpu.SemaphoreType.DMA((3,)),
+            pltpu.SemaphoreType.DMA((5,)),
             pltpu.SemaphoreType.DMA((3,)),
         ],
         compiler_params=pltpu.CompilerParams(
@@ -737,31 +791,7 @@
             vmem_limit_bytes=VMEM_LIMIT,
         ),
         name="exchange_last" if last else "exchange_first",
-    )(frame_sums, point_sums, state, own)
-
-
-def emit_kernel(poses, points, poses_out, points_out, sems):
-    copies = [
-        pltpu.make_async_copy(poses, poses_out, sems.at[0]),
-        pltpu.make_async_copy(points, points_out, sems.at[1]),
-    ]
-    for copy in copies:
-        copy.start()
-    for copy in copies:
-        copy.wait()
-
-
-def emit(poses, points):
-    far = pl.BlockSpec(memory_space=pl.ANY)
-    return pl.pallas_call(
-        emit_kernel,
-        in_specs=[far] * 2,
-        out_specs=[far] * 2,
-        out_shape=[jax.ShapeDtypeStruct(a.shape, a.dtype) for a in (poses, points)],
-        scratch_shapes=[pltpu.SemaphoreType.DMA((2,))],
-        compiler_params=pltpu.CompilerParams(vmem_limit_bytes=VMEM_LIMIT),
-        name="emit",
-    )(poses, points)
+    )(frame_sums, point_sums, state, links, own)
 
 
 def on_device(
@@ -776,16 +806,17 @@
     block_slot,
 ):
     rows, count = lax.axis_size("tm"), lax.axis_size("lm")
-    state, own, window, packed = prepare(
+    state, links, own, window, packed = prepare(
         camera_poses, odometry, odometry_info, landmarks, observations, count
     )
-    for iteration in range(ITERS):
-        frame_sums, point_sums = tile_sums(
-            state, window, packed, tile_frame, tile_block, tile_count, block_slot
-        )
-        last = iteration == ITERS - 1
-        state, own, window = exchange(frame_sums, point_sums, state, own, count, rows, last)
-    return tuple(emit(state, own))
+    for iteration in range(ITERS - 1):
+        sums = tile_sums(state, window, packed, tile_frame, tile_block, tile_count, block_slot)
+        state, own, window = exchange(*sums, state, links, own, count, rows, False)
+    sums = tile_sums(state, window, packed, tile_frame, tile_block, tile_count, block_slot)
+    poses, pose_step, points, point_step = exchange(
+        *sums, state, links, own, count, rows, True
+    )
+    return (poses - pose_step, points - point_step)
 
 
 def solution(mesh):

time: 56.8 us -> 54.8 us (0.965)
  Pallas kernels: 55.4 us -> 50.6 us
  other arithmetic: 0 us -> 2.71 us
    sub x0 -> x2, other arithmetic: none -> 2.71 us  [on_device(): return (poses - pose_step, points - point_step)]
    pallas_call x1 -> x0, Pallas kernels: 2.36 us -> none  [emit(): pl.pallas_call(emit_kernel, in_specs=[far] * 2, out_specs=[far] * 2, out_...]
    pallas_call x2, Pallas kernels: 18.5 us -> 16.2 us  [tile_sums(): pl.pallas_call(functools.partial(tiles_kernel, chunks, unroll), in_specs=...]
    pallas_call x1, Pallas kernels: 11.5 us -> 10 us  [prepare(): pl.pallas_call(functools.partial(prepare_kernel, count), out_shape=[jax.S...]
    pallas_call x2, Pallas kernels: 23.1 us -> 24.4 us  [exchange(): pl.pallas_call(functools.partial(exchange_kernel, count, rows, last), out...]
where the time goes in v5:
time: 54.8 us; the launch traced here: 54.6 us
  Pallas kernels  50.6 us (92%)
  other arithmetic  2.71 us (5%)
  between operations  1.32 us (2%)
    pallas_call x2, Pallas kernels, exchange(): pl.pallas_call(functools.partial(exchange_kernel, count, rows, last), out...  24.4 us
    pallas_call x2, Pallas kernels, tile_sums(): pl.pallas_call(functools.partial(tiles_kernel, chunks, unroll), in_specs=...  16.2 us
    pallas_call x1, Pallas kernels, prepare(): pl.pallas_call(functools.partial(prepare_kernel, count), out_shape=[jax.S...  10 us
    sub x2, other arithmetic, on_device(): return (poses - pose_step, points - point_step)  2.71 us

profile of v5, /device:TPU:0, one launch (start us, length us, event | category | flops | bytes accessed | tf_op | source)
XLA Modules:
  0.0 54.6 jit_solution(13102722524338457362)
XLA Ops:
  1.3 10.0 %prepare.1 = (f32[16,8,64]{2,1,0:T(8,128)}, f32[16,8,64]{2,1,0:T(8,128)}, f32[8,256]{1,0:T(8,128)}, f32[32,256]{1,0:T(8,128)}, f32[3,96,32,128]{3,2,1,0:T(8,128)}) custom-call(f32[6,1024]{1,0:T(8,128)} %camera_poses.1, f32[6,1024]{1,0:T(8,128)} %odometry.1, f32[1,1024]{1,0:T(1,128)} %bitcast.3, f32[3,512]{1,0:T(4,128)} %landmarks.1, ...), custom_call_target="tpu_custom_call" | custom-call | tf_op jit(solution)/shard_map/prepare/pallas_call | solution.py:443
  11.3 8.1 %tile_sums.2 = (f32[16,16,128]{2,1,0:T(8,128)}, f32[32,8,128]{2,1,0:T(8,128)}) custom-call(s32[96]{0:T(128)} %frame_list_far.3, s32[96]{0:T(128)} %block_list_far.3, s32[1]{0:T(128)S(6)} %copy.11.count_far, s32[1,32]{1,0:T(1,128)} %slot_far.3, f32[16,8,64]{2,1,0:T(8,128)} %get-tuple-element.18.poses_far.state_far, f32[32,256]{1,0:T(8,128)} %get-tuple-element.19.window_far, ...), custom_call_target="tpu_custom_call" | custom-call | tf_op jit(solution)/shard_map/tile_sums/pallas_call | solution.py:287
  19.4 12.3 %exchange_first.1 = (f32[16,8,64]{2,1,0:T(8,128)}, f32[8,256]{1,0:T(8,128)}, f32[32,256]{1,0:T(8,128)}) custom-call(f32[16,16,128]{2,1,0:T(8,128)} %get-tuple-element.21.frame_far, f32[32,8,128]{2,1,0:T(8,128)} %get-tuple-element.22.point_far, f32[16,8,64]{2,1,0:T(8,128)} %get-tuple-element.18.poses_far.state_far, f32[16,8,64]{2,1,0:T(8,128)} %get-tuple-element.23.links_far, ...), custom_call_target="tpu_custom_call" | custom-call | tf_op jit(solution)/shard_map/exchange_first/pallas_call | solution.py:766
  31.7 8.1 %tile_sums.3 = (f32[16,16,128]{2,1,0:T(8,128)}, f32[32,8,128]{2,1,0:T(8,128)}) custom-call(s32[96]{0:T(128)} %frame_list_far.3, s32[96]{0:T(128)} %block_list_far.3, s32[1]{0:T(128)S(6)} %copy.11.count_far, s32[1,32]{1,0:T(1,128)} %slot_far.3, f32[16,8,64]{2,1,0:T(8,128)} %get-tuple-element.25.poses_far.state_far, f32[32,256]{1,0:T(8,128)} %get-tuple-element.26.window_far, ...), custom_call_target="tpu_custom_call" | custom-call | tf_op jit(solution)/shard_map/tile_sums/pallas_call | solution.py:287
  39.8 12.1 %exchange_last.1 = (f32[6,1024]{1,0:T(8,128)}, f32[6,1024]{1,0:T(8,128)}, f32[3,512]{1,0:T(4,128)}, f32[3,512]{1,0:T(4,128)}) custom-call(f32[16,16,128]{2,1,0:T(8,128)} %get-tuple-element.27.frame_far, f32[32,8,128]{2,1,0:T(8,128)} %get-tuple-element.28.point_far, f32[16,8,64]{2,1,0:T(8,128)} %get-tuple-element.25.poses_far.state_far, ...), custom_call_target="tpu_custom_call" | custom-call | tf_op jit(solution)/shard_map/exchange_last/pallas_call | solution.py:766
  51.9 1.4 %sub.6 = f32[6,1024]{1,0:T(8,128)} subtract(f32[6,1024]{1,0:T(8,128)} %get-tuple-element.30, f32[6,1024]{1,0:T(8,128)} %get-tuple-element.31) | non-fusion elementwise | flops 6144 | bytes 73728 | tf_op jit(solution)/shard_map/sub | solution.py:819
  53.3 1.3 %sub.7 = f32[3,512]{1,0:T(4,128)} subtract(f32[3,512]{1,0:T(4,128)} %get-tuple-element.32, f32[3,512]{1,0:T(4,128)} %get-tuple-element.33) | non-fusion elementwise | flops 1536 | bytes 18432 | tf_op jit(solution)/shard_map/sub | solution.py:819

commit v6 on v5

--- a/solution.py
+++ b/solution.py
@@ -176,9 +176,9 @@
 
     window_copy.wait()
 
-    @pl.loop(0, point_blocks, step=4)
+    @pl.loop(0, point_blocks, step=8)
     def _(start):
-        for u in range(4):
+        for u in range(8):
             block = start + u
             line = window[pl.ds(block, 1), :]
             both = []
@@ -193,9 +193,9 @@
 
     pose_copy.wait()
 
-    @pl.loop(0, frame_blocks, step=2)
+    @pl.loop(0, frame_blocks, step=4)
     def _(start):
-        for u in range(2):
+        for u in range(4):
             block = start + u
             mine = poses[block, 0:8, :]
             rows = frame_features(mine, sub, lane)
@@ -342,16 +342,23 @@
 
 def prepare_kernel(
     count,
+    poses_far,
+    odometry_far,
+    info_far,
+    landmarks_far,
+    obs_far,
+    state_out,
+    links_out,
+    own_out,
+    window_out,
+    packed_far,
     camera_poses,
     odometry,
     odometry_info,
     landmarks,
-    obs_far,
     state,
     links,
     own,
-    window,
-    packed_far,
     obs,
     packed,
     send_sem,
@@ -364,13 +371,33 @@
     blocks = own.shape[0]
     frame_blocks = state.shape[0]
     slots = obs.shape[3]
+    own_rows = pl.ds(pl.multiple_of(me * blocks, blocks), blocks)
     loads = [
-        pltpu.make_async_copy(obs_far.at[k], obs.at[k], load_sem.at[k]) for k in range(3)
+        pltpu.make_async_copy(source, target, load_sem.at[n])
+        for n, (source, target) in enumerate(
+            (
+                (obs_far.at[0], obs.at[0]),
+                (landmarks_far, landmarks),
+                (poses_far, camera_poses),
+                (odometry_far, odometry),
+                (info_far, odometry_info),
+                (obs_far.at[1], obs.at[1]),
+                (obs_far.at[2], obs.at[2]),
+            )
+        )
     ]
     for load in loads:
         load.start()
-    own_rows = pl.ds(pl.multiple_of(me * blocks, blocks), blocks)
+    stores = []
+
+    def store(source, target):
+        stores.append(pltpu.make_async_copy(source, target, store_sem.at[len(stores)]))
+        stores[-1].start()
+
     own[...] = jnp.zeros_like(own)
+    state[...] = jnp.zeros_like(state)
+    links[...] = jnp.zeros_like(links)
+    loads[1].wait()
     for block in range(blocks):
         for k in range(3):
             own[block : block + 1, k * TILE : (k + 1) * TILE] = landmarks[
@@ -382,7 +409,7 @@
         copies.append(
             pltpu.make_async_remote_copy(
                 src_ref=own,
-                dst_ref=window.at[own_rows],
+                dst_ref=window_out.at[own_rows],
                 send_sem=send_sem.at[d],
                 recv_sem=recv_sem.at[d],
                 device_id=(row, peer),
@@ -390,21 +417,23 @@
             )
         )
         copies[-1].start()
-    window[own_rows] = own[...]
-    state[...] = jnp.zeros_like(state)
-    links[...] = jnp.zeros_like(links)
+    store(own, window_out.at[own_rows])
+    store(own, own_out)
+    for load in loads[2:5]:
+        load.wait()
     for block in range(frame_blocks):
         here = slice(block * TILE, (block + 1) * TILE)
         state[block, 0:6, :] = camera_poses[:, here]
         links[block, 0:6, :] = odometry[:, here]
         links[block, 6:7, :] = odometry_info[:, here]
+    store(state, state_out)
+    store(links, links_out)
 
     row_id = lax.broadcasted_iota(jnp.int32, (slots, slots), 0)
     column_id = lax.broadcasted_iota(jnp.int32, (slots, slots), 1)
     identity = jnp.where(row_id == column_id, 1.0, 0.0).astype(jnp.bfloat16)
-    stores = []
     for k in range(3):
-        loads[k].wait()
+        loads[(0, 5, 6)[k]].wait()
 
         @pl.loop(0, HALF, step=8)
         def _(start):
@@ -424,10 +453,7 @@
             here = pl.ds(pl.multiple_of(start, 8), 8)
             packed[k, :, here, :] = jnp.swapaxes(jnp.stack(turned), 0, 1)
 
-        stores.append(
-            pltpu.make_async_copy(packed.at[k], packed_far.at[k], store_sem.at[k])
-        )
-        stores[-1].start()
+        store(packed.at[k], packed_far.at[k])
     for copy in copies + stores:
         copy.wait()
 
@@ -437,33 +463,33 @@
     frame_blocks = camera_poses.shape[1] // TILE
     blocks = landmarks.shape[1] // TILE
     by_tile = jnp.transpose(observations, (1, 2, 3, 0))
-    vmem = pl.BlockSpec(memory_space=pltpu.VMEM)
     far = pl.BlockSpec(memory_space=pl.ANY)
+    info = odometry_info[None, :]
+    inputs = (camera_poses, odometry, info, landmarks, by_tile)
+    state_shape = (frame_blocks, 8, TILE)
+    own_shape = (blocks, 4 * TILE)
     packed_shape = (3, slots, HALF, 128)
+    shapes = [state_shape, state_shape, own_shape, (blocks * count, 4 * TILE), packed_shape]
     return pl.pallas_call(
         functools.partial(prepare_kernel, count),
-        out_shape=[
-            jax.ShapeDtypeStruct((frame_blocks, 8, TILE), jnp.float32),
-            jax.ShapeDtypeStruct((frame_blocks, 8, TILE), jnp.float32),
-            jax.ShapeDtypeStruct((blocks, 4 * TILE), jnp.float32),
-            jax.ShapeDtypeStruct((blocks * count, 4 * TILE), jnp.float32),
-            jax.ShapeDtypeStruct(packed_shape, jnp.float32),
-        ],
-        in_specs=[vmem] * 4 + [far],
-        out_specs=[vmem] * 4 + [far],
-        scratch_shapes=[
+        out_shape=[jax.ShapeDtypeStruct(shape, jnp.float32) for shape in shapes],
+        in_specs=[far] * 5,
+        out_specs=[far] * 5,
+        scratch_shapes=[pltpu.VMEM(a.shape, jnp.float32) for a in inputs[:4]]
+        + [pltpu.VMEM(shape, jnp.float32) for shape in shapes[:3]]
+        + [
             pltpu.VMEM(by_tile.shape, jnp.bfloat16),
             pltpu.VMEM(packed_shape, jnp.float32),
             pltpu.SemaphoreType.DMA((count - 1,)),
             pltpu.SemaphoreType.DMA((count - 1,)),
-            pltpu.SemaphoreType.DMA((3,)),
-            pltpu.SemaphoreType.DMA((3,)),
+            pltpu.SemaphoreType.DMA((7,)),
+            pltpu.SemaphoreType.DMA((7,)),
         ],
         compiler_params=pltpu.CompilerParams(
             collective_id=0, has_side_effects=True, vmem_limit_bytes=VMEM_LIMIT
         ),
         name="prepare",
-    )(camera_poses, odometry, odometry_info[None, :], landmarks, by_tile)
+    )(*inputs)
 
 
 def pose_update(total, state, links, before, links_before, after, final):
@@ -556,7 +582,8 @@
 
 
 def exchange_kernel(count, rows, last, frame_far, point_far, state_far, links_far, own_far, *refs):
-    outs, refs = (refs[:4], refs[4:]) if last else (refs[:3], refs[3:])
+    pose_out, own_out = refs[:2]
+    window_out = None if last else refs[2]
     (
         frame_in,
         point_in,
@@ -565,7 +592,6 @@
         extended_links,
         own,
         fresh,
-        gathered,
         fresh_points,
         send_sem,
         recv_sem,
@@ -573,7 +599,7 @@
         edge_recv,
         load_sem,
         store_sem,
-    ) = refs
+    ) = refs[2 if last else 3 :]
     row = lax.axis_index("tm")
     me, peers = ring_peers(count)
     frame_blocks = state_far.shape[0]
@@ -647,12 +673,6 @@
     extended_links[0] = jnp.zeros_like(extended_links[0])
     for load in loads:
         load.wait()
-    if last:
-        for pair in range(frame_blocks // 2):
-            outs[0][:, pair * 128 : (pair + 1) * 128] = jnp.concatenate(
-                [extended[2 * pair + 1, 0:6, :], extended[2 * pair + 2, 0:6, :]], axis=1
-            )
-
     @pl.when(row > 0)
     def _():
         edge(0, row - 1).wait_recv()
@@ -692,56 +712,30 @@
         frame_total, mine, mine_links, before, links_before, after, final
     )
     points, point_step = point_update(point_total, own[...])
-    window_copies, stores = [], []
-    if last:
-        gathered[here] = jnp.zeros_like(mine)
-        for k in range(6):
-            gathered[here, k, :] = pose_step[k]
-        pose_copies = [
-            send(2, d, peer, gathered.at[here], gathered.at[here])
-            for d, peer in enumerate(peers)
-        ]
-        for k in range(3):
-            for out, value in ((outs[2], points[k]), (outs[3], point_step[k])):
-                for pair in range(own_blocks // 2):
-                    out[k : k + 1, pair * 128 : (pair + 1) * 128] = jnp.concatenate(
-                        [value[2 * pair : 2 * pair + 1], value[2 * pair + 1 : 2 * pair + 2]],
-                        axis=1,
-                    )
-    else:
-        pose_out, own_out, window_out = outs
-        fresh[...] = mine
-        for k in range(6):
-            fresh[:, k, :] = poses[k] - pose_step[k]
-        pose_copies = [
-            send(2, d, peer, fresh, pose_out.at[here]) for d, peer in enumerate(peers)
-        ]
-        fresh_points[...] = own[...]
-        for k in range(3):
-            fresh_points[:, k * TILE : (k + 1) * TILE] = points[k] - point_step[k]
-        window_copies = [
+    fresh[...] = mine
+    for k in range(6):
+        fresh[:, k, :] = poses[k] - pose_step[k]
+    gathers = [send(2, d, peer, fresh, pose_out.at[here]) for d, peer in enumerate(peers)]
+    fresh_points[...] = own[...]
+    for k in range(3):
+        fresh_points[:, k * TILE : (k + 1) * TILE] = points[k] - point_step[k]
+    targets = [(fresh, pose_out.at[here]), (fresh_points, own_out)]
+    if not last:
+        gathers += [
             send(3, d, peer, fresh_points, window_out.at[here_points])
             for d, peer in enumerate(peers)
         ]
-        for n, (source, target) in enumerate(
-            (
-                (fresh, pose_out.at[here]),
-                (fresh_points, window_out.at[here_points]),
-                (fresh_points, own_out),
-            )
-        ):
-            stores.append(pltpu.make_async_copy(source, target, store_sem.at[n]))
-            stores[-1].start()
-
+        targets.append((fresh_points, window_out.at[here_points]))
+    stores = [
+        pltpu.make_async_copy(source, target, store_sem.at[n])
+        for n, (source, target) in enumerate(targets)
+    ]
+    for copy in stores:
+        copy.start()
     for copy in frame_copies + point_copies:
         copy.wait_send()
-    for copy in pose_copies + window_copies + stores:
+    for copy in gathers + stores:
         copy.wait()
-    if last:
-        for pair in range(frame_blocks // 2):
-            outs[1][:, pair * 128 : (pair + 1) * 128] = jnp.concatenate(
-                [gathered[2 * pair, 0:6, :], gathered[2 * pair + 1, 0:6, :]], axis=1
-            )
 
     @pl.when(row < rows - 1)
     def _():
@@ -757,17 +751,15 @@
     frame_blocks = state.shape[0]
     own_blocks = own.shape[0]
     share = frame_blocks // count
-    vmem = pl.BlockSpec(memory_space=pltpu.VMEM)
     far = pl.BlockSpec(memory_space=pl.ANY)
-    if last:
-        shapes = [(6, frame_blocks * TILE)] * 2 + [(3, own_blocks * TILE)] * 2
-    else:
-        shapes = [state.shape, own.shape, (own_blocks * count,) + own.shape[1:]]
+    shapes = [state.shape, own.shape]
+    if not last:
+        shapes.append((own_blocks * count,) + own.shape[1:])
     return pl.pallas_call(
         functools.partial(exchange_kernel, count, rows, last),
         out_shape=[jax.ShapeDtypeStruct(shape, jnp.float32) for shape in shapes],
         in_specs=[far] * 5,
-        out_specs=[vmem if last else far] * len(shapes),
+        out_specs=[far] * len(shapes),
         scratch_shapes=[
             pltpu.VMEM((count, share, 16, 128), jnp.float32),
             pltpu.VMEM((count, own_blocks, 8, 128), jnp.float32),
@@ -776,7 +768,6 @@
             pltpu.VMEM((frame_blocks + 2, 8, TILE), jnp.float32),
             pltpu.VMEM(own.shape, jnp.float32),
             pltpu.VMEM((share, 8, TILE), jnp.float32),
-            pltpu.VMEM((frame_blocks, 8, TILE), jnp.float32),
             pltpu.VMEM(own.shape, jnp.float32),
             pltpu.SemaphoreType.DMA((4, count - 1)),
             pltpu.SemaphoreType.DMA((4, count - 1)),
@@ -792,6 +783,34 @@
         ),
         name="exchange_last" if last else "exchange_first",
     )(frame_sums, point_sums, state, links, own)
+
+
+def emit_kernel(state, own, poses, points):
+    for pair in range(state.shape[0] // 2):
+        here = slice(pair * 128, (pair + 1) * 128)
+        poses[:, here] = jnp.concatenate(
+            [state[2 * pair, 0:6, :], state[2 * pair + 1, 0:6, :]], axis=1
+        )
+    for pair in range(own.shape[0] // 2):
+        here = slice(pair * 128, (pair + 1) * 128)
+        for k in range(3):
+            part = own[2 * pair : 2 * pair + 2, k * TILE : (k + 1) * TILE]
+            points[k : k + 1, here] = jnp.concatenate([part[0:1], part[1:2]], axis=1)
+
+
+def emit(state, own):
+    vmem = pl.BlockSpec(memory_space=pltpu.VMEM)
+    return pl.pallas_call(
+        emit_kernel,
+        in_specs=[vmem] * 2,
+        out_specs=[vmem] * 2,
+        out_shape=[
+            jax.ShapeDtypeStruct((6, state.shape[0] * TILE), jnp.float32),
+            jax.ShapeDtypeStruct((3, own.shape[0] * TILE), jnp.float32),
+        ],
+        compiler_params=pltpu.CompilerParams(vmem_limit_bytes=VMEM_LIMIT),
+        name="emit",
+    )(state, own)
 
 
 def on_device(
@@ -813,10 +832,8 @@
         sums = tile_sums(state, window, packed, tile_frame, tile_block, tile_count, block_slot)
         state, own, window = exchange(*sums, state, links, own, count, rows, False)
     sums = tile_sums(state, window, packed, tile_frame, tile_block, tile_count, block_slot)
-    poses, pose_step, points, point_step = exchange(
-        *sums, state, links, own, count, rows, True
-    )
-    return (poses - pose_step, points - point_step)
+    state, own = exchange(*sums, state, links, own, count, rows, True)
+    return tuple(emit(state, own))
 
 
 def solution(mesh):

time: 54.8 us -> 50.7 us (0.925)
  other arithmetic: 2.71 us -> 0 us
  Pallas kernels: 50.6 us -> 49.4 us
    pallas_call x2, Pallas kernels: 24.4 us -> 18.3 us  [exchange(): pl.pallas_call(functools.partial(exchange_kernel, count, rows, last), out...]
    pallas_call x2, Pallas kernels: 16.2 us -> 19.9 us  [tile_sums(): pl.pallas_call(functools.partial(tiles_kernel, chunks, unroll), in_specs=...]
    sub x2 -> x0, other arithmetic: 2.71 us -> none  [on_device(): return (poses - pose_step, points - point_step)]
    pallas_call x0 -> x1, Pallas kernels: none -> 1.55 us  [emit(): pl.pallas_call(emit_kernel, in_specs=[vmem] * 2, out_specs=[vmem] * 2, ou...]
where the time goes in v6:
time: 50.7 us
  Pallas kernels  49.4 us (97%)
  between operations  1.32 us (3%)
    pallas_call x2, Pallas kernels, tile_sums(): pl.pallas_call(functools.partial(tiles_kernel, chunks, unroll), in_specs=...  19.9 us
    pallas_call x2, Pallas kernels, exchange(): pl.pallas_call(functools.partial(exchange_kernel, count, rows, last), out...  18.3 us
    pallas_call x1, Pallas kernels, prepare(): pl.pallas_call(functools.partial(prepare_kernel, count), out_shape=[jax.S...  9.7 us
    pallas_call x1, Pallas kernels, emit(): pl.pallas_call(emit_kernel, in_specs=[vmem] * 2, out_specs=[vmem] * 2, ou...  1.55 us

profile of v6, /device:TPU:0, one launch (start us, length us, event | category | flops | bytes accessed | tf_op | source)
XLA Modules:
  0.0 50.7 jit_solution(5026078118750453141)
XLA Ops:
  1.3 9.7 %prepare.1 = (f32[16,8,64]{2,1,0:T(8,128)}, f32[16,8,64]{2,1,0:T(8,128)}, f32[8,256]{1,0:T(8,128)}, f32[32,256]{1,0:T(8,128)}, f32[3,96,32,128]{3,2,1,0:T(8,128)}) custom-call(f32[6,1024]{1,0:T(8,128)} %poses_far.1, f32[6,1024]{1,0:T(8,128)} %odometry_far.1, f32[1,1024]{1,0:T(1,128)} %bitcast.3, f32[3,512]{1,0:T(4,128)} %landmarks_far.1, ...), custom_call_target="tpu_custom_call" | custom-call | tf_op jit(solution)/shard_map/prepare/pallas_call | solution.py:473
  11.0 9.9 %tile_sums.2 = (f32[16,16,128]{2,1,0:T(8,128)}, f32[32,8,128]{2,1,0:T(8,128)}) custom-call(s32[96]{0:T(128)} %frame_list_far.3, s32[96]{0:T(128)} %block_list_far.3, s32[1]{0:T(128)S(6)} %copy.11.count_far, s32[1,32]{1,0:T(1,128)} %slot_far.3, f32[16,8,64]{2,1,0:T(8,128)} %get-tuple-element.16.poses_far.state_far, f32[32,256]{1,0:T(8,128)} %get-tuple-element.17.window_far, ...), custom_call_target="tpu_custom_call" | custom-call | tf_op jit(solution)/shard_map/tile_sums/pallas_call | solution.py:287
  20.9 8.8 %exchange_first.1 = (f32[16,8,64]{2,1,0:T(8,128)}, f32[8,256]{1,0:T(8,128)}, f32[32,256]{1,0:T(8,128)}) custom-call(f32[16,16,128]{2,1,0:T(8,128)} %get-tuple-element.19.frame_far, f32[32,8,128]{2,1,0:T(8,128)} %get-tuple-element.20.point_far, f32[16,8,64]{2,1,0:T(8,128)} %get-tuple-element.16.poses_far.state_far, f32[16,8,64]{2,1,0:T(8,128)} %get-tuple-element.21.links_far, ...), custom_call_target="tpu_custom_call" | custom-call | tf_op jit(solution)/shard_map/exchange_first/pallas_call | solution.py:758
  29.8 9.9 %tile_sums.3 = (f32[16,16,128]{2,1,0:T(8,128)}, f32[32,8,128]{2,1,0:T(8,128)}) custom-call(s32[96]{0:T(128)} %frame_list_far.3, s32[96]{0:T(128)} %block_list_far.3, s32[1]{0:T(128)S(6)} %copy.11.count_far, s32[1,32]{1,0:T(1,128)} %slot_far.3, f32[16,8,64]{2,1,0:T(8,128)} %get-tuple-element.23.poses_far.state_far, f32[32,256]{1,0:T(8,128)} %get-tuple-element.24.window_far, ...), custom_call_target="tpu_custom_call" | custom-call | tf_op jit(solution)/shard_map/tile_sums/pallas_call | solution.py:287
  39.7 9.4 %exchange_last.1 = (f32[16,8,64]{2,1,0:T(8,128)}, f32[8,256]{1,0:T(8,128)}) custom-call(f32[16,16,128]{2,1,0:T(8,128)} %get-tuple-element.25.frame_far, f32[32,8,128]{2,1,0:T(8,128)} %get-tuple-element.26.point_far, f32[16,8,64]{2,1,0:T(8,128)} %get-tuple-element.23.poses_far.state_far, f32[16,8,64]{2,1,0:T(8,128)} %get-tuple-element.21.links_far, ...), custom_call_target="tpu_custom_call" | custom-call | tf_op jit(solution)/shard_map/exchange_last/pallas_call | solution.py:758
  49.2 1.5 %emit.1 = (f32[6,1024]{1,0:T(8,128)}, f32[3,512]{1,0:T(4,128)}) custom-call(f32[16,8,64]{2,1,0:T(8,128)} %get-tuple-element.28.state, f32[8,256]{1,0:T(8,128)} %get-tuple-element.29.own), custom_call_target="tpu_custom_call" | custom-call | tf_op jit(solution)/shard_map/emit/pallas_call | solution.py:803

commit v7 on v6

--- a/solution.py
+++ b/solution.py
@@ -227,7 +227,9 @@
         squared = (
             residual[0] * residual[0] + residual[1] * residual[1] + residual[2] * residual[2]
         )
-        weight = jnp.where(live, 1.0, 0.0) / (1.0 + squared * (1.0 / robust_scale))
+        divisor = 1.0 + squared * (1.0 / robust_scale)
+        weight = pl.reciprocal(divisor, approx=True)
+        weight = jnp.where(live, 1.0, 0.0) * (weight * (2.0 - divisor * weight))
         images = jnp.concatenate(
             [weight] + [weight * measured[k] for k in range(3)], axis=0
         )
@@ -492,7 +494,19 @@
     )(*inputs)
 
 
-def pose_update(total, state, links, before, links_before, after, final):
+def link_terms(state, links, before, links_before, after, final):
+    current = [state[:, k, :] for k in range(6)]
+    weight_before = links_before[:, 6, :]
+    weight_after = jnp.where(final, 0.0, links[:, 6, :])
+    link_grad = []
+    for k in range(6):
+        ahead = after[:, k, :] - current[k] - links[:, k, :]
+        behind = current[k] - before[:, k, :] - links_before[:, k, :]
+        link_grad.append(weight_before * behind - weight_after * ahead)
+    return current, link_grad, weight_after + weight_before + damping
+
+
+def pose_update(total, current, link_grad, diagonal_add):
     def both(row_low, row_high, start):
         return jnp.concatenate(
             [total[:, row_low, start : start + HALF], total[:, row_high, start : start + HALF]],
@@ -507,7 +521,6 @@
     def lever(a, k):
         return both(1 + a, 5 + a, HALF * (1 + k))
 
-    current = [state[:, k, :] for k in range(6)]
     w, t = current[0:3], current[3:6]
     turned = cross_product(w, centroid)
     grad_off = [centroid[k] + turned[k] + t[k] * counted - seen[k] for k in range(3)]
@@ -526,15 +539,6 @@
         )
         grad_rot.append(trace * w[k] - product + pushed[k] - (lever(a, b) - lever(b, a)))
 
-    weight_before = links_before[:, 6, :]
-    weight_after = jnp.where(final, 0.0, links[:, 6, :])
-    link_grad = []
-    for k in range(6):
-        ahead = after[:, k, :] - current[k] - links[:, k, :]
-        behind = current[k] - before[:, k, :] - links_before[:, k, :]
-        link_grad.append(weight_before * behind - weight_after * ahead)
-    diagonal_add = weight_after + weight_before + damping
-
     zero_entry = jnp.zeros_like(counted)
     rotation_block = [
         [moments[1] + moments[2] + diagonal_add, -moments[3], -moments[4]],
@@ -552,7 +556,7 @@
         matrix.append([cross_block[k][i] for k in range(3)] + offset_row)
     sums = grad_rot + grad_off
     step = block_solve(matrix, [sums[k] + link_grad[k] for k in range(6)])
-    return current, step
+    return step
 
 
 def point_update(total, own):
@@ -702,15 +706,17 @@
         row == rows - 1, frame_blocks * TILE - 1, -1
     )
 
+    poses, link_grad, diagonal_add = link_terms(
+        mine, mine_links, before, links_before, after, final
+    )
+
     for copy in frame_copies + point_copies:
         copy.wait_recv()
     frame_total, point_total = frame_in[count - 1], point_in[count - 1]
     for d in range(count - 1):
         frame_total = frame_total + frame_in[d]
         point_total = point_total + point_in[d]
-    poses, pose_step = pose_update(
-        frame_total, mine, mine_links, before, links_before, after, final
-    )
+    pose_step = pose_update(frame_total, poses, link_grad, diagonal_add)
     points, point_step = point_update(point_total, own[...])
     fresh[...] = mine
     for k in range(6):

time: 50.7 us -> 50.9 us (level)
    pallas_call x2, Pallas kernels: 18.3 us -> 19.7 us  [exchange(): pl.pallas_call(functools.partial(exchange_kernel, count, rows, last), out...]
    pallas_call x2, Pallas kernels: 19.9 us -> 18.8 us  [tile_sums(): pl.pallas_call(functools.partial(tiles_kernel, chunks, unroll), in_specs=...]
where the time goes in v7:
time: 50.9 us; the launch traced here: 51.1 us
  Pallas kernels  49.7 us (98%)
  between operations  1.32 us (3%)
    pallas_call x2, Pallas kernels, exchange(): pl.pallas_call(functools.partial(exchange_kernel, count, rows, last), out...  19.7 us
    pallas_call x2, Pallas kernels, tile_sums(): pl.pallas_call(functools.partial(tiles_kernel, chunks, unroll), in_specs=...  18.8 us
    pallas_call x1, Pallas kernels, prepare(): pl.pallas_call(functools.partial(prepare_kernel, count), out_shape=[jax.S...  9.7 us
    pallas_call x1, Pallas kernels, emit(): pl.pallas_call(emit_kernel, in_specs=[vmem] * 2, out_specs=[vmem] * 2, ou...  1.55 us

profile of v7, /device:TPU:0, one launch (start us, length us, event | category | flops | bytes accessed | tf_op | source)
XLA Modules:
  0.0 51.1 jit_solution(17427487922214307910)
XLA Ops:
  1.3 9.7 %prepare.1 = (f32[16,8,64]{2,1,0:T(8,128)}, f32[16,8,64]{2,1,0:T(8,128)}, f32[8,256]{1,0:T(8,128)}, f32[32,256]{1,0:T(8,128)}, f32[3,96,32,128]{3,2,1,0:T(8,128)}) custom-call(f32[6,1024]{1,0:T(8,128)} %poses_far.1, f32[6,1024]{1,0:T(8,128)} %odometry_far.1, f32[1,1024]{1,0:T(1,128)} %bitcast.3, f32[3,512]{1,0:T(4,128)} %landmarks_far.1, ...), custom_call_target="tpu_custom_call" | custom-call | tf_op jit(solution)/shard_map/prepare/pallas_call | solution.py:475
  11.0 9.4 %tile_sums.2 = (f32[16,16,128]{2,1,0:T(8,128)}, f32[32,8,128]{2,1,0:T(8,128)}) custom-call(s32[96]{0:T(128)} %frame_list_far.3, s32[96]{0:T(128)} %block_list_far.3, s32[1]{0:T(128)S(6)} %copy.11.count_far, s32[1,32]{1,0:T(1,128)} %slot_far.3, f32[16,8,64]{2,1,0:T(8,128)} %get-tuple-element.16.poses_far.state_far, f32[32,256]{1,0:T(8,128)} %get-tuple-element.17.window_far, ...), custom_call_target="tpu_custom_call" | custom-call | tf_op jit(solution)/shard_map/tile_sums/pallas_call | solution.py:289
  20.4 10.2 %exchange_first.1 = (f32[16,8,64]{2,1,0:T(8,128)}, f32[8,256]{1,0:T(8,128)}, f32[32,256]{1,0:T(8,128)}) custom-call(f32[16,16,128]{2,1,0:T(8,128)} %get-tuple-element.19.frame_far, f32[32,8,128]{2,1,0:T(8,128)} %get-tuple-element.20.point_far, f32[16,8,64]{2,1,0:T(8,128)} %get-tuple-element.16.poses_far.state_far, f32[16,8,64]{2,1,0:T(8,128)} %get-tuple-element.21.links_far, ...), custom_call_target="tpu_custom_call" | custom-call | tf_op jit(solution)/shard_map/exchange_first/pallas_call | solution.py:764
  30.6 9.4 %tile_sums.3 = (f32[16,16,128]{2,1,0:T(8,128)}, f32[32,8,128]{2,1,0:T(8,128)}) custom-call(s32[96]{0:T(128)} %frame_list_far.3, s32[96]{0:T(128)} %block_list_far.3, s32[1]{0:T(128)S(6)} %copy.11.count_far, s32[1,32]{1,0:T(1,128)} %slot_far.3, f32[16,8,64]{2,1,0:T(8,128)} %get-tuple-element.23.poses_far.state_far, f32[32,256]{1,0:T(8,128)} %get-tuple-element.24.window_far, ...), custom_call_target="tpu_custom_call" | custom-call | tf_op jit(solution)/shard_map/tile_sums/pallas_call | solution.py:289
  40.0 9.5 %exchange_last.1 = (f32[16,8,64]{2,1,0:T(8,128)}, f32[8,256]{1,0:T(8,128)}) custom-call(f32[16,16,128]{2,1,0:T(8,128)} %get-tuple-element.25.frame_far, f32[32,8,128]{2,1,0:T(8,128)} %get-tuple-element.26.point_far, f32[16,8,64]{2,1,0:T(8,128)} %get-tuple-element.23.poses_far.state_far, f32[16,8,64]{2,1,0:T(8,128)} %get-tuple-element.21.links_far, ...), custom_call_target="tpu_custom_call" | custom-call | tf_op jit(solution)/shard_map/exchange_last/pallas_call | solution.py:764
  49.5 1.5 %emit.1 = (f32[6,1024]{1,0:T(8,128)}, f32[3,512]{1,0:T(4,128)}) custom-call(f32[16,8,64]{2,1,0:T(8,128)} %get-tuple-element.28.state, f32[8,256]{1,0:T(8,128)} %get-tuple-element.29.own), custom_call_target="tpu_custom_call" | custom-call | tf_op jit(solution)/shard_map/emit/pallas_call | solution.py:809
